TPU v7x, 256 devices: a whole 4x4x8 slice. The times are simulated.
256 devices in a mesh: gx: 16 (over z, core), yz: 16 (over y, x).
Axes of the slice: x: 4, y: 4, z: 8, core: 2. Of those that a mesh axis runs over, the one named last changes fastest.
Arguments:
- loads: float32 [16, 294912], P(None, ('gx', 'yz')), may hold values from -30 to 30
- stiffness: bfloat16 [294912, 1152], P(('gx', 'yz')), may hold values from -1 to 16, as said below
- local_inverse: bfloat16 [294912, 1152], P(('gx', 'yz')), may hold values from -1 to 2, as said below
- coarse_basis: bfloat16 [24, 294912], P(None, ('gx', 'yz')), may hold values from -0.1875 to 0.1875
- coarse_inverse: bfloat16 [1024, 1024], replicated, may hold values from -1 to 2, as said below
- primal_index: int32 [256, 24], P(('gx', 'yz')), may hold values from 0 to 1023, as said below
- layer_counts: int32 [256, 2], P(('gx', 'yz')), may hold values from 0 to 144, as said below
- layer_index: int32 [256, 2, 144], P(('gx', 'yz')), may hold values from 0 to 1151, as said below
- across_counts: int32 [256, 16], P(('gx', 'yz')), may hold values from 0 to 48, as said below
- across_index: int32 [256, 16, 48], P(('gx', 'yz')), may hold values from 0 to 1151, as said below
Outputs:
- solution: float32 [16, 294912], P(None, ('gx', 'yz'))
- residual: float32 [16, 294912], P(None, ('gx', 'yz'))
- precond: float32 [16, 294912], P(None, ('gx', 'yz'))
Inputs may be any that keep to these rules, and one draw needn't show every extreme that they name: `stiffness`: each subdomain's block of 1152 rows is symmetric positive definite. `local_inverse`: each subdomain's block of 1152 rows is symmetric positive definite. `coarse_inverse`: symmetric positive definite. `primal_index`: the 24 entries of one subdomain are distinct. layer_counts[s, 1] equals layer_counts[s + 16, 0]; the lower count is 0 on the first layer and the upper count 0 on the last; for one position p across, drawn afresh, every two adjacent layers share exactly 144 dofs there. `layer_index`: entry j of subdomain s's upper list and entry j of subdomain s + 16's lower list name the same shared dof; entries past a count are 0; all list entries of one subdomain, layer and across lists together, are distinct. across_counts[g * 16 + p, q] equals across_counts[g * 16 + q, p]; it is 0 for q = p, exactly 48 for q = p + 1 and q = p - 1 (mod 16), and in each layer one subdomain shares exactly 48 with every other one. `across_index`: entry j of subdomain s's list toward t and entry j of t's list toward s name the same shared dof; entries past a count are 0.
All inputs are finite; a program needn't handle non-finite values.
Results may differ from a plain program's by a relative error of at most 0.025.
Values may be sent and summed in bfloat16 or wider, within the bound.
A program may use at most 64 MiB of HBM per device.

v0:
```python
import jax
import jax.numpy as jnp
from jax import lax
from jax.sharding import PartitionSpec as P

ITERS = 2


def extended(value, sides, width):
    for axis, dim in sides:
        count, length = (lax.axis_size(axis), value.shape[dim])
        up = [(i, (i + 1) % count) for i in range(count - 1)]
        down = [(j, i) for i, j in up]
        last = lax.slice_in_dim(value, length - width, length, axis=dim)
        initial = lax.slice_in_dim(value, 0, width, axis=dim)
        before = lax.ppermute(last, axis, up)
        after = lax.ppermute(initial, axis, down)
        value = jnp.concatenate([before, value, after], axis=dim)
    return value


def inner_product(left, right):
    return lax.dot_general(
        left,
        right,
        (((1,), (1,)), ((), ())),
        precision=lax.Precision.HIGHEST,
        preferred_element_type=jnp.float32,
    )


def spd_solve(matrix, right_side):
    lower = jnp.linalg.cholesky(matrix)
    middle = lax.linalg.triangular_solve(lower, right_side, left_side=True, lower=True)
    return lax.linalg.triangular_solve(lower, middle, left_side=True, lower=True, transpose_a=True)


def assemble(vector, lists):
    layer_list, layer_mask, across_list, across_mask = lists
    cases = vector.shape[0]
    outgoing = jnp.take(vector, layer_list, axis=1) * layer_mask[None]
    framed = extended(outgoing, (("gx", 1),), 1)
    sending = jnp.take(vector, across_list, axis=1) * across_mask[None]
    arrived = lax.all_to_all(
        sending.astype(jnp.bfloat16), "yz", split_axis=1, concat_axis=1, tiled=True
    ).astype(sending.dtype)
    summed = vector.at[:, across_list.reshape(-1)].add(arrived.reshape(cases, -1))
    summed = summed.at[:, layer_list[0]].add(framed[:, 0])
    return summed.at[:, layer_list[1]].add(framed[:, 3])


def dof_weight(length, lists):
    layer_list, layer_mask, across_list, across_mask = lists
    shared = jnp.zeros((length,), jnp.float32)
    shared = shared.at[layer_list.reshape(-1)].add(layer_mask.reshape(-1))
    shared = shared.at[across_list.reshape(-1)].add(across_mask.reshape(-1))
    return 1.0 / (1.0 + shared)


def precondition(residual, weight, local_inverse, coarse_basis, coarse_inverse, primal, lists):
    weighted = (weight[None] * residual).astype(jnp.bfloat16)
    local_part = jnp.dot(weighted, local_inverse, preferred_element_type=jnp.float32)
    coarse_terms = lax.dot_general(
        weighted, coarse_basis, (((1,), (1,)), ((), ())), preferred_element_type=jnp.float32
    )
    coarse_size = coarse_inverse.shape[0]
    selector = (primal[:, None] == jnp.arange(coarse_size)[None, :]).astype(jnp.float32)
    spread = jnp.dot(coarse_terms, selector, precision=lax.Precision.HIGHEST)
    coarse_total = lax.psum(spread, ("gx", "yz"))
    coarse_rhs = coarse_total.astype(jnp.bfloat16)
    row_count = coarse_size // lax.axis_size("gx")
    row_block = lax.dynamic_slice_in_dim(
        coarse_inverse, lax.axis_index("gx") * row_count, row_count, 0
    )
    own_rows = lax.dot_general(
        coarse_rhs, row_block, (((1,), (1,)), ((), ())), preferred_element_type=jnp.float32
    ).astype(jnp.bfloat16)
    coarse_solution = lax.all_gather(own_rows, "gx", axis=1, tiled=True)
    picked = jnp.take(coarse_solution, primal, axis=1)
    coarse_part = jnp.dot(picked, coarse_basis, preferred_element_type=jnp.float32)
    assembled = assemble(weight[None] * (local_part + coarse_part), lists)
    gram = lax.psum(inner_product(weight[None] * assembled, residual), ("gx", "yz"))
    return (assembled, gram)


def per_device(
    loads,
    stiffness,
    local_inverse,
    coarse_basis,
    coarse_inverse,
    primal_index,
    layer_counts,
    layer_index,
    across_counts,
    across_index,
):
    layer_list = layer_index[0]
    across_list = across_index[0]
    layer_mask = (jnp.arange(layer_list.shape[1])[None, :] < layer_counts[0][:, None]).astype(
        jnp.float32
    )
    across_mask = (jnp.arange(across_list.shape[1])[None, :] < across_counts[0][:, None]).astype(
        jnp.float32
    )
    lists = (layer_list, layer_mask, across_list, across_mask)
    weight = dof_weight(loads.shape[1], lists)
    primal = primal_index[0]

    def apply_preconditioner(current):
        return precondition(
            current, weight, local_inverse, coarse_basis, coarse_inverse, primal, lists
        )

    residual = assemble(loads, lists)
    solution = jnp.zeros_like(residual)
    precond, product = apply_preconditioner(residual)
    direction = precond
    for iteration in range(ITERS):
        stiff_image = jnp.dot(
            direction.astype(jnp.bfloat16), stiffness, preferred_element_type=jnp.float32
        )
        curvature = lax.psum(inner_product(direction, stiff_image), ("gx", "yz"))
        image = assemble(stiff_image, lists)
        alpha = spd_solve(curvature, product)
        solution = solution + jnp.dot(alpha.T, direction, precision=lax.Precision.HIGHEST)
        residual = residual - jnp.dot(alpha.T, image, precision=lax.Precision.HIGHEST)
        precond, product_next = apply_preconditioner(residual)
        if iteration + 1 < ITERS:
            beta = spd_solve(product, product_next)
            direction = precond + jnp.dot(beta.T, direction, precision=lax.Precision.HIGHEST)
        product = product_next
    return (solution, residual, precond)


def solution(mesh):
    in_specs = (
        P(None, ("gx", "yz")),
        P(("gx", "yz"), None),
        P(("gx", "yz"), None),
        P(None, ("gx", "yz")),
        P(),
        P(("gx", "yz"), None),
        P(("gx", "yz"), None),
        P(("gx", "yz"), None, None),
        P(("gx", "yz"), None),
        P(("gx", "yz"), None, None),
    )
    out_specs = (P(None, ("gx", "yz")), P(None, ("gx", "yz")), P(None, ("gx", "yz")))
    return jax.shard_map(
        per_device, mesh=mesh, in_specs=in_specs, out_specs=out_specs, check_vma=False
    )
```

profile of v0, /device:TPU:1, one launch (start us, length us, event | category | flops | bytes accessed | tf_op | source)
XLA Modules:
  0.0 816.1 jit_solution(10036473766111364378)
XLA Ops:
  5.4 5.1 collective-permute-start.1
  18.3 6.5 all-to-all-start
  29.4 5.6 scatter_fusion
  35.5 7.8 scatter_fusion.1
  52.0 79.3 %psum.49 = bf16[16,1024]{1,0:T(8,128)(2,1)S(1)} all-reduce(f32[16,1024]{1,0:T(8,128)S(1)} %fusion.19), channel_id=1, replica_groups=mesh['gx'=16,'yz'=16] {'gx','yz'}, use_global_device_ids=true, to_apply=%region_5.8 | all-reduce | flops 16384 | bytes 98304 | tf_op jit(solution)/shard_map/psum | solution.py:69
  132.4 17.2 %all-gather = bf16[16,64,16]{1,2,0:T(8,128)(2,1)S(1)} all-gather(bf16[1,64,16]{1,2,0:T(8,128)(2,1)S(1)} %fusion.3), channel_id=1, replica_groups=mesh['gx'=16,'yz'=16] {'gx'}, dimensions={0}, use_global_device_ids=true | all-gather | bytes 34816 | tf_op jit(solution)/shard_map/all_gather | solution.py:78
  173.3 7.4 scatter_fusion.2
  197.5 75.7 %all-reduce = (f32[16,16]{0,1:T(8,128)S(1)}, f32[16,16]{0,1:T(8,128)S(1)}) all-reduce(f32[16,16]{0,1:T(8,128)S(1)} %fusion.46, f32[16,16]{0,1:T(8,128)} %fusion.117), channel_id=1, replica_groups=mesh['gx'=16,'yz'=16] {'gx','yz'}, use_global_device_ids=true, to_apply=%region_12.17 | all-reduce | flops 512 | bytes 4096 | tf_op jit(solution)/shard_map/psum | solution.py:82
  294.9 6.0 all-to-all-done.2
  303.6 8.2 scatter_fusion.3
  322.3 73.2 %psum.52 = bf16[16,1024]{1,0:T(8,128)(2,1)} all-reduce(f32[16,1024]{1,0:T(8,128)S(1)} %fusion.18), channel_id=1, replica_groups=mesh['gx'=16,'yz'=16] {'gx','yz'}, use_global_device_ids=true, to_apply=%region_16.0 | all-reduce | flops 16384 | bytes 98304 | tf_op jit(solution)/shard_map/psum | solution.py:69
  396.5 17.2 %all-gather.1 = bf16[16,64,16]{1,2,0:T(8,128)(2,1)S(1)} all-gather(bf16[1,64,16]{1,2,0:T(8,128)(2,1)S(1)} %fusion.4), channel_id=1, replica_groups=mesh['gx'=16,'yz'=16] {'gx'}, dimensions={0}, use_global_device_ids=true | all-gather | bytes 34816 | tf_op jit(solution)/shard_map/all_gather | solution.py:78
  441.8 4.1 all-to-all-done.3
  448.6 8.2 %scatter_fusion.4 = f32[16,1152]{0,1:T(8,128)} fusion(f32[16,1152]{0,1:T(8,128)} %copy.152, s32[768]{0:T(1024)S(1)} %fusion.94, f32[768,16]{1,0:T(8,128)} %copy.153), kind=kCustom, calls=%fused_computation.26 | custom fusion | flops 12288 | bytes 150528 | tf_op jit(solution)/shard_map/scatter-add | solution.py:47
  465.4 72.5 %psum.53 = f32[16,16]{1,0:T(8,128)S(1)} all-reduce(f32[16,16]{1,0:T(8,128)S(1)} %fusion.44), channel_id=1, replica_groups=mesh['gx'=16,'yz'=16] {'gx','yz'}, use_global_device_ids=true, to_apply=%region_20.27 | all-reduce | flops 256 | bytes 2048 | tf_op jit(solution)/shard_map/psum | solution.py:82
  549.5 73.6 %psum.54 = f32[16,16]{0,1:T(8,128)S(1)} all-reduce(f32[16,16]{0,1:T(8,128)} %fusion.118), channel_id=1, replica_groups=mesh['gx'=16,'yz'=16] {'gx','yz'}, use_global_device_ids=true, to_apply=%region_21.28 | all-reduce | flops 256 | bytes 2048 | tf_op jit(solution)/shard_map/psum | solution.py:123
  639.9 4.4 all-to-all-start.4
  645.3 5.5 all-to-all-done.4
  654.2 8.2 %scatter_fusion.5 = f32[16,1152]{0,1:T(8,128)} fusion(f32[16,1152]{0,1:T(8,128)} %copy.163, s32[768]{0:T(1024)S(1)} %fusion.94, f32[768,16]{1,0:T(8,128)} %copy.164), kind=kCustom, calls=%fused_computation.29 | custom fusion | flops 12288 | bytes 150528 | tf_op jit(solution)/shard_map/scatter-add | solution.py:47
  673.3 73.7 %psum.55 = bf16[16,1024]{1,0:T(8,128)(2,1)} all-reduce(f32[16,1024]{1,0:T(8,128)} %fusion.17), channel_id=1, replica_groups=mesh['gx'=16,'yz'=16] {'gx','yz'}, use_global_device_ids=true, to_apply=%region_25.32 | all-reduce | flops 16384 | bytes 98304 | tf_op jit(solution)/shard_map/psum | solution.py:69
  748.1 17.6 %all-gather.2 = bf16[16,64,16]{1,2,0:T(8,128)(2,1)} all-gather(bf16[1,64,16]{1,2,0:T(8,128)(2,1)S(1)} %fusion.5), channel_id=1, replica_groups=mesh['gx'=16,'yz'=16] {'gx'}, dimensions={0}, use_global_device_ids=true | all-gather | bytes 34816 | tf_op jit(solution)/shard_map/all_gather | solution.py:78
  788.5 3.7 all-to-all-start.5
  794.2 4.4 all-to-all-done.5
  799.1 7.8 scatter_fusion.6
  (229 shorter events, 221.7 us)
Async XLA Ops:
  0.6 149.0 %copy-start = (bf16[1152,1152]{1,0:T(8,128)(2,1)S(1)}, bf16[1152,1152]{1,0:T(8,128)(2,1)}, u32[]{:S(2)}) copy-start(bf16[1152,1152]{1,0:T(8,128)(2,1)} %param.23) | copy-start | bytes 7962628
  0.7 24.8 %copy-start.6 = (s32[1,16,48]{2,1,0:T(8,128)S(1)}, s32[1,16,48]{2,1,0:T(8,128)}, u32[]{:S(2)}) copy-start(s32[1,16,48]{2,1,0:T(8,128)} %param.30) | copy-start | bytes 9220
  5.4 41.5 %collective-permute-start.1 = (f32[16,1,144]{0,2,1:T(8,128)}, f32[16,1,144]{0,2,1:T(8,128)}, u32[]{:S(2)}, u32[]{:S(2)}) collective-permute-start(f32[16,1,144]{0,2,1:T(8,128)} %get-tuple-element.33), channel_id=1, source_target_pairs={{16,0},{32,16},{48,32},{64,48},{80,64},{96,80},{112,96},{128,112},... | collective-permute-start | bytes 27656 | tf_op jit(solution)/shard_map/ppermute | solution.py:17
  10.5 32.7 %collective-permute-start = (f32[16,1,144]{0,2,1:T(8,128)}, f32[16,1,144]{0,2,1:T(8,128)}, u32[]{:S(2)}, u32[]{:S(2)}) collective-permute-start(f32[16,1,144]{0,2,1:T(8,128)} %get-tuple-element.34), channel_id=1, source_target_pairs={{0,16},{16,32},{32,48},{48,64},{64,80},{80,96},{96,112},{112,128},... | collective-permute-start | bytes 27656 | tf_op jit(solution)/shard_map/ppermute | solution.py:16
  18.3 16.8 %all-to-all-start = ((bf16[16,2,384]{2,1,0:T(2,128)(2,1)}), bf16[16,2,384]{2,1,0:T(2,128)(2,1)S(1)}, u32[]{:S(2)}, u32[]{:S(2)}) async-start(bf16[16,2,384]{2,1,0:T(2,128)(2,1)} %reshape.687), calls=%async_computation | async-start | bytes 49152 | tf_op jit(solution)/shard_map/all_to_all | solution.py:44
  35.0 115.2 %copy-start.11 = (s32[1024]{0:T(1024)}, s32[1024]{0:T(1024)S(1)}, u32[]{:S(2)}) copy-start(s32[1024]{0:T(1024)S(1)} %pad_clamp_fusion) | copy-start | bytes 12292
  46.8 104.0 %copy-start.14 = (pred[24]{0:T(512)(128)(4,1)S(1)}, pred[24]{0:T(512)(128)(4,1)}, u32[]{:S(2)}) copy-start(pred[24]{0:T(512)(128)(4,1)} %compare_and_fusion.2) | copy-start | bytes 76
  160.5 10.0 %all-to-all-start.1 = ((bf16[16,2,384]{2,1,0:T(2,128)(2,1)}), bf16[16,2,384]{2,1,0:T(2,128)(2,1)S(1)}, u32[]{:S(2)}, u32[]{:S(2)}) async-start(bf16[16,2,384]{2,1,0:T(2,128)(2,1)} %reshape.689), calls=%async_computation.1 | async-start | bytes 49152 | tf_op jit(solution)/shard_map/all_to_all | solution.py:44
  165.6 15.0 %collective-permute-start.2 = (f32[16,1,144]{0,2,1:T(8,128)}, f32[16,1,144]{0,2,1:T(8,128)}, u32[]{:S(2)}, u32[]{:S(2)}) collective-permute-start(f32[16,1,144]{0,2,1:T(8,128)} %get-tuple-element.32), channel_id=1, source_target_pairs={{0,16},{16,32},{32,48},{48,64},{64,80},{80,96},{96,112},{112,128},... | collective-permute-start | bytes 27656 | tf_op jit(solution)/shard_map/ppermute | solution.py:16
  167.5 15.2 %collective-permute-start.3 = (f32[16,1,144]{0,2,1:T(8,128)}, f32[16,1,144]{0,2,1:T(8,128)}, u32[]{:S(2)}, u32[]{:S(2)}) collective-permute-start(f32[16,1,144]{0,2,1:T(8,128)} %get-tuple-element.31), channel_id=1, source_target_pairs={{16,0},{32,16},{48,32},{64,48},{80,64},{96,80},{112,96},{128,112},... | collective-permute-start | bytes 27656 | tf_op jit(solution)/shard_map/ppermute | solution.py:17
  277.7 43.0 %copy-start.4 = (f32[16,16]{1,0:T(8,128)}, f32[16,16]{1,0:T(8,128)S(1)}, u32[]{:S(2)}) copy-start(f32[16,16]{1,0:T(8,128)S(1)} %fusion.79) | copy-start | bytes 3076
  281.0 34.4 %collective-permute-start.5 = (f32[16,1,144]{0,2,1:T(8,128)}, f32[16,1,144]{0,2,1:T(8,128)}, u32[]{:S(2)}, u32[]{:S(2)}) collective-permute-start(f32[16,1,144]{0,2,1:T(8,128)} %get-tuple-element.29), channel_id=1, source_target_pairs={{16,0},{32,16},{48,32},{64,48},{80,64},{96,80},{112,96},{128,112},... | collective-permute-start | bytes 27656 | tf_op jit(solution)/shard_map/ppermute | solution.py:17
  283.7 28.1 %collective-permute-start.4 = (f32[16,1,144]{0,2,1:T(8,128)}, f32[16,1,144]{0,2,1:T(8,128)}, u32[]{:S(2)}, u32[]{:S(2)}) collective-permute-start(f32[16,1,144]{0,2,1:T(8,128)} %get-tuple-element.30), channel_id=1, source_target_pairs={{0,16},{16,32},{32,48},{48,64},{64,80},{80,96},{96,112},{112,128},... | collective-permute-start | bytes 27656 | tf_op jit(solution)/shard_map/ppermute | solution.py:16
  290.8 10.1 %all-to-all-start.2 = ((bf16[16,2,384]{2,1,0:T(2,128)(2,1)}), bf16[16,2,384]{2,1,0:T(2,128)(2,1)S(1)}, u32[]{:S(2)}, u32[]{:S(2)}) async-start(bf16[16,2,384]{2,1,0:T(2,128)(2,1)} %reshape.691), calls=%async_computation.2 | async-start | bytes 49152 | tf_op jit(solution)/shard_map/all_to_all | solution.py:44
  426.7 33.7 %collective-permute-start.7 = (f32[16,1,144]{0,2,1:T(8,128)}, f32[16,1,144]{0,2,1:T(8,128)}, u32[]{:S(2)}, u32[]{:S(2)}) collective-permute-start(f32[16,1,144]{0,2,1:T(8,128)} %get-tuple-element.27), channel_id=1, source_target_pairs={{16,0},{32,16},{48,32},{64,48},{80,64},{96,80},{112,96},{128,112},... | collective-permute-start | bytes 27656 | tf_op jit(solution)/shard_map/ppermute | solution.py:17
  428.8 28.0 %collective-permute-start.6 = (f32[16,1,144]{0,2,1:T(8,128)}, f32[16,1,144]{0,2,1:T(8,128)}, u32[]{:S(2)}, u32[]{:S(2)}) collective-permute-start(f32[16,1,144]{0,2,1:T(8,128)} %get-tuple-element.28), channel_id=1, source_target_pairs={{0,16},{16,32},{32,48},{48,64},{64,80},{80,96},{96,112},{112,128},... | collective-permute-start | bytes 27656 | tf_op jit(solution)/shard_map/ppermute | solution.py:16
  435.8 10.1 %all-to-all-start.3 = ((bf16[16,2,384]{2,1,0:T(2,128)(2,1)}), bf16[16,2,384]{2,1,0:T(2,128)(2,1)S(1)}, u32[]{:S(2)}, u32[]{:S(2)}) async-start(bf16[16,2,384]{2,1,0:T(2,128)(2,1)} %reshape.693), calls=%async_computation.3 | async-start | bytes 49152 | tf_op jit(solution)/shard_map/all_to_all | solution.py:44
  630.6 35.3 %collective-permute-start.9 = (f32[16,1,144]{0,2,1:T(8,128)}, f32[16,1,144]{0,2,1:T(8,128)}, u32[]{:S(2)}, u32[]{:S(2)}) collective-permute-start(f32[16,1,144]{0,2,1:T(8,128)} %get-tuple-element.25), channel_id=1, source_target_pairs={{16,0},{32,16},{48,32},{64,48},{80,64},{96,80},{112,96},{128,112},... | collective-permute-start | bytes 27656 | tf_op jit(solution)/shard_map/ppermute | solution.py:17
  633.2 29.2 %collective-permute-start.8 = (f32[16,1,144]{0,2,1:T(8,128)}, f32[16,1,144]{0,2,1:T(8,128)}, u32[]{:S(2)}, u32[]{:S(2)}) collective-permute-start(f32[16,1,144]{0,2,1:T(8,128)} %get-tuple-element.26), channel_id=1, source_target_pairs={{0,16},{16,32},{32,48},{48,64},{64,80},{80,96},{96,112},{112,128},... | collective-permute-start | bytes 27656 | tf_op jit(solution)/shard_map/ppermute | solution.py:16
  639.9 10.8 %all-to-all-start.4 = ((bf16[16,2,384]{2,1,0:T(2,128)(2,1)}), bf16[16,2,384]{2,1,0:T(2,128)(2,1)}, u32[]{:S(2)}, u32[]{:S(2)}) async-start(bf16[16,2,384]{2,1,0:T(2,128)(2,1)} %reshape.695), calls=%async_computation.4 | async-start | bytes 49152 | tf_op jit(solution)/shard_map/all_to_all | solution.py:44
  671.2 108.1 %copy-start.3 = (f32[16,1152]{1,0:T(8,128)}, f32[16,1152]{1,0:T(8,128)S(1)}, u32[]{:S(2)}) copy-start(f32[16,1152]{1,0:T(8,128)S(1)} %convolution_subtract_fusion) | copy-start | bytes 221188
  781.0 29.4 %collective-permute-start.11 = (f32[16,1,144]{0,2,1:T(8,128)}, f32[16,1,144]{0,2,1:T(8,128)}, u32[]{:S(2)}, u32[]{:S(2)}) collective-permute-start(f32[16,1,144]{0,2,1:T(8,128)} %get-tuple-element.23), channel_id=1, source_target_pairs={{16,0},{32,16},{48,32},{64,48},{80,64},{96,80},{112,96},{128,112},... | collective-permute-start | bytes 27656 | tf_op jit(solution)/shard_map/ppermute | solution.py:17
  783.1 23.8 %collective-permute-start.10 = (f32[16,1,144]{0,2,1:T(8,128)}, f32[16,1,144]{0,2,1:T(8,128)}, u32[]{:S(2)}, u32[]{:S(2)}) collective-permute-start(f32[16,1,144]{0,2,1:T(8,128)} %get-tuple-element.24), channel_id=1, source_target_pairs={{0,16},{16,32},{32,48},{48,64},{64,80},{80,96},{96,112},{112,128},... | collective-permute-start | bytes 27656 | tf_op jit(solution)/shard_map/ppermute | solution.py:16
  788.5 10.2 %all-to-all-start.5 = ((bf16[16,2,384]{2,1,0:T(2,128)(2,1)}), bf16[16,2,384]{2,1,0:T(2,128)(2,1)S(1)}, u32[]{:S(2)}, u32[]{:S(2)}) async-start(bf16[16,2,384]{2,1,0:T(2,128)(2,1)} %reshape.697), calls=%async_computation.5 | async-start | bytes 49152 | tf_op jit(solution)/shard_map/all_to_all | solution.py:44
  (11 other events, 178.4 us)
where the time goes:
time: 829 us; the launch traced here: 816 us
  blocking collectives  500 us (60%)
  other arithmetic  122 us (15%)
  local copies, waits for them, and re-layouts  83 us (10%)
  starting transfers between devices  60.3 us (7%)
  matrix products  28.6 us (3%)
  waiting for transfers between devices  20.1 us (2%)
    psum x3, blocking collectives, precondition(): coarse_total = lax.psum(spread, ('gx', 'yz'))  226 us
    psum x2, blocking collectives, precondition(): lax.psum(inner_product(weight[None] * assembled, residual), ('gx', 'yz'))  148 us
    psum x1, blocking collectives, per_device(): curvature = lax.psum(inner_product(direction, stiff_image), ('gx', 'yz'))  73.6 us
    all_gather x3, blocking collectives, precondition(): coarse_solution = lax.all_gather(own_rows, 'gx', axis=1, tiled=True)  52 us
    scatter-add x6, other arithmetic, assemble(): vector.at[:, across_list.reshape(-1)].add(arrived.reshape(cases, -1))  47.4 us
    gather x12, local copies, waits for them, and re-layouts, assemble(): sending = jnp.take(vector, across_list, axis=1) * across_mask[None]  27.3 us
    all_to_all x6, starting transfers between devices, assemble(): lax.all_to_all(sending.astype(jnp.bfloat16), 'yz', split_axis=1, concat_a...  25.1 us
    all_to_all x6, waiting for transfers between devices, assemble(): lax.all_to_all(sending.astype(jnp.bfloat16), 'yz', split_axis=1, concat_a...  20 us
  transfers between devices with their start and end apart: 18, of which 4 were waited for; matrix products, arithmetic and copies ran while one was open for 14% of the time, Pallas kernels for 0%

commit v1 on v0

v1 whole, which is shorter than its diff:
```python
import functools

import jax
import jax.numpy as jnp
from jax import lax
from jax.experimental import pallas as pl
from jax.experimental.pallas import tpu as pltpu
from jax.sharding import PartitionSpec as P

MESH = pl.DeviceIdType.MESH
F32, BF16 = jnp.float32, jnp.bfloat16

CASES = 16
IFACE = 1152
PRIMAL = 24
SLOTS = 48
FACE = 144
COARSE = 1024
RING = 16
TILES = 11
LANES = 128
NSLOT = TILES * LANES
PACKED = 512


def dot(a, b):
    return jnp.dot(a, b, preferred_element_type=F32)


def dot_nt(a, b):
    return lax.dot_general(a, b, (((1,), (1,)), ((), ())), preferred_element_type=F32)


def split(x):
    hi = x.astype(BF16)
    return hi, (x - hi.astype(F32)).astype(BF16)


def iota(shape, dim):
    return lax.broadcasted_iota(jnp.int32, shape, dim)


def fold(m):
    lane = iota((8, LANES), 1)
    return jnp.where(lane < 64, m[0:8], pltpu.roll(m[8:16], 64, 1))


def unfold(m):
    return jnp.concatenate([m, pltpu.roll(m, 64, 1)], axis=0)


def pack(tiles):
    lane = iota((8, LANES), 1)
    keep = (lane % 64) < 32
    pairs = []
    for i in range(8):
        even = jnp.where(keep, tiles[2 * i], 0.0)
        odd = jnp.where(keep, tiles[2 * i + 1], 0.0)
        pairs.append(even + pltpu.roll(odd, 32, 1))
    columns = []
    for i in range(4):
        a, b = pairs[2 * i], pairs[2 * i + 1]
        top = jnp.where(lane < 64, a, pltpu.roll(b, 64, 1))
        low = jnp.where(lane < 64, pltpu.roll(a, 64, 1), b)
        columns.append(jnp.concatenate([top, low], axis=0))
    return jnp.concatenate(columns, axis=1)


def eliminate(m, base):
    rows = iota((CASES, LANES), 0)
    for k in range(CASES):
        row = m[k : k + 1, :]
        scaled = row * (1.0 / row[:, base + k : base + k + 1])
        m = jnp.where(rows == k, scaled, m - m[:, base + k : base + k + 1] * scaled)
    return m


def lanes_of(m, start):
    lane = iota(m.shape, 1)
    return jnp.where((lane >= start) & (lane < start + CASES), m, 0.0)


def split3(x):
    a = x.astype(BF16)
    rest = x - a.astype(F32)
    b = rest.astype(BF16)
    return a, b, (rest - b.astype(F32)).astype(BF16)


def factor_t(m, start):
    a, b, c = (part.astype(F32) for part in split3(m))
    stack = jnp.concatenate([a, a, a, b, b, c, jnp.zeros((LANES - 6 * CASES, LANES), F32)], axis=0)
    return jnp.transpose(stack)[start : start + CASES, :].astype(BF16)


def apply_t(left, v):
    a, b, c = split3(v)
    pad = jnp.zeros((LANES - 6 * CASES, v.shape[1]), BF16)
    return dot(left, jnp.concatenate([a, b, c, a, b, a, pad], axis=0))


def kernel(
    loads, stiff_hbm, linv_hbm, basis, cinv_hbm, primal, lcounts, lindex, acounts, aindex,
    sol_out, res_out, pre_out,
    stiff, linv, cinv, gather, scatter, basis_rows, basis_cols, weight, table,
    idx, lidx, local, terms0, img,
    slot_s, slot_r, face_r, gram_s, gram_r, col_s, col_r, pk_s, pk_r, pidx_s, pidx_r, pcol_s, pcol_r,
    load_sem, slot_ss, slot_rs, face_ss, face_rs, gram_ss, gram_rs, col_ss, col_rs, pk_ss, pk_rs, px_ss, px_rs,
):
    gx, yz = lax.axis_index("gx"), lax.axis_index("yz")
    y, x = yz // 4, yz % 4
    offsets = sorted(
        [(a, b) for a in range(4) for b in range(4) if (a, b) != (0, 0)],
        key=lambda o: -(min(o[0], 4 - o[0]) + min(o[1], 4 - o[1])),
    )
    peers = [((y + a) % 4) * 4 + (x + b) % 4 for a, b in offsets]
    zs = sorted(range(1, RING), key=lambda o: -min(o, RING - o))
    columns = [(gx + o) % RING for o in zs]

    barrier = pltpu.get_barrier_semaphore()
    for q in peers:
        pl.semaphore_signal(barrier, 1, device_id=(gx, q), device_id_type=MESH)
    for q in columns:
        pl.semaphore_signal(barrier, 1, device_id=(q, yz), device_id_type=MESH)

    loading = [
        pltpu.make_async_copy(cinv_hbm, cinv, load_sem.at[0]),
        pltpu.make_async_copy(linv_hbm, linv, load_sem.at[1]),
        pltpu.make_async_copy(stiff_hbm, stiff, load_sem.at[2]),
    ]
    for copy in loading:
        copy.start()

    def to_peers(src, dst, ssem, rsem):
        for q in peers:
            pltpu.make_async_remote_copy(src(q), dst, ssem, rsem, device_id=(gx, q), device_id_type=MESH).start()

    def to_columns(src, dst, ssem, rsem):
        for q in columns:
            pltpu.make_async_remote_copy(src, dst, ssem, rsem, device_id=(q, yz), device_id_type=MESH).start()

    def wait_bytes(ref, sem):
        pltpu.make_async_copy(ref, ref, sem).wait()

    lane1 = iota((1, LANES), 1)
    idx[...] = jnp.full((LANES, LANES), -1, jnp.int32)
    lidx[...] = jnp.full((24, LANES), -1, jnp.int32)
    slot_lane = iota((1, SLOTS), 1)
    for q in range(RING):
        lidx[q : q + 1, 0:SLOTS] = jnp.where(slot_lane < acounts[0:1, q : q + 1], aindex[0, q : q + 1, :], -1)
    lane8 = iota((8, LANES), 1)
    idx[0:8, :] = jnp.where(lane8 < 64, lidx[0:8, :], pltpu.roll(lidx[8:16, :], 64, 1))
    face_lane = iota((1, FACE), 1)
    low = jnp.where(face_lane < lcounts[0:1, 0:1], lindex[0, 0:1, :], -1)
    up = jnp.where(face_lane < lcounts[0:1, 1:2], lindex[0, 1:2, :], -1)
    lidx[16:17, 0 : FACE - LANES] = low[:, LANES:FACE]
    lidx[17:18, 0 : FACE - LANES] = up[:, LANES:FACE]
    idx[8:9, :] = low[:, 0:LANES]
    idx[9:10, :] = jnp.where(lane1 < 64, lidx[16:17, :], pltpu.roll(lidx[17:18, :], 64, 1))
    idx[10:11, :] = up[:, 0:LANES]
    lidx[18:19, 0:PRIMAL] = primal[...]
    prow = lidx[18:19, :]

    row_iota = iota((IFACE, LANES), 0)
    for b in range(TILES):
        gather[:, b * LANES : (b + 1) * LANES] = jnp.where(row_iota == idx[b : b + 1, :], 1.0, 0.0).astype(BF16)
    idx_cols = jnp.transpose(idx[...].astype(F32))
    lane_iota = iota((LANES, IFACE), 1).astype(F32)
    for b in range(TILES):
        scatter[b * LANES : (b + 1) * LANES, :] = jnp.where(idx_cols[:, b : b + 1] == lane_iota, 1.0, 0.0).astype(BF16)
    weight[...] = 1.0 / (1.0 + dot(jnp.ones((CASES, NSLOT), BF16), scatter[...]))

    basis_pad = jnp.concatenate([basis[...].astype(F32), jnp.zeros((LANES - PRIMAL, IFACE), F32)], axis=0)
    basis_rows[...] = basis_pad.astype(BF16)
    basis_cols[...] = jnp.transpose(basis_pad).astype(BF16)

    prow8 = jnp.broadcast_to(prow.astype(F32), (8, LANES))
    pidx_s[...] = jnp.where(lane8 < 32, prow8, jnp.where((lane8 >= 64) & (lane8 < 96), pltpu.roll(prow8, 64, 1), 0.0))

    for phase in range(6):
        slot_r[phase, pl.ds(yz, 1)] = jnp.zeros((1, CASES, LANES), BF16)

    pl.semaphore_wait(barrier, len(peers) + len(columns))

    below, above = (gx + RING - 1) % RING, (gx + 1) % RING

    def exchange_start(phase, values):
        out = dot(values, gather[...]).astype(BF16)
        for b in range(TILES):
            slot_s[phase, b] = out[:, b * LANES : (b + 1) * LANES]
        to_peers(lambda q: slot_s.at[phase, q % 8], slot_r.at[phase, yz], slot_ss.at[phase], slot_rs.at[phase])
        pltpu.make_async_remote_copy(
            slot_s.at[phase, pl.ds(8, 2)], face_r.at[phase, 1], face_ss.at[phase], face_rs.at[phase],
            device_id=(below, yz), device_id_type=MESH,
        ).start()
        pltpu.make_async_remote_copy(
            slot_s.at[phase, pl.ds(9, 2)], face_r.at[phase, 0], face_ss.at[phase], face_rs.at[phase],
            device_id=(above, yz), device_id_type=MESH,
        ).start()

    def exchange_finish(phase):
        wait_bytes(face_r.at[phase], face_rs.at[phase])
        wait_bytes(slot_r.at[phase, pl.ds(0, 15)], slot_rs.at[phase])
        lane = iota((CASES, LANES), 1)
        first = yz < 8
        mine = (lane < 64) == first
        parts = []
        for b in range(8):
            a, c = slot_r[phase, b].astype(F32), slot_r[phase, b + 8].astype(F32)
            stay = jnp.where(first, a, c)
            move = jnp.where(first, c, a)
            parts.append(jnp.where(mine, stay, pltpu.roll(move, 64, 1)))
        parts.append(face_r[phase, 0, 1].astype(F32))
        tails = jnp.where(lane < 64, face_r[phase, 1, 1].astype(F32), face_r[phase, 0, 0].astype(F32))
        parts.append(pltpu.roll(tails, 64, 1))
        parts.append(face_r[phase, 1, 0].astype(F32))
        return dot(jnp.concatenate(parts, axis=1).astype(BF16), scatter[...])

    def coarse_terms(weighted):
        hi, lo = split(weighted)
        both = dot(jnp.concatenate([hi, lo], axis=0), basis_cols[...])
        return fold(both[0:CASES] + both[CASES:])

    def columns_start(phase, count):
        to_columns(
            col_s.at[phase, pl.ds(0, count)], col_r.at[phase, gx, pl.ds(0, count)], col_ss.at[phase], col_rs.at[phase]
        )

    def columns_wait(phase, count):
        wait_bytes(col_r.at[phase, pl.ds(0, 15), pl.ds(0, count)], col_rs.at[phase])

    def packed_start(phase, values):
        out = values.astype(BF16)
        pk_s[phase] = out
        pk_r[phase, pl.ds(yz, 1)] = out[None]
        to_peers(lambda q: pk_s.at[phase], pk_r.at[phase, yz], pk_ss.at[phase], pk_rs.at[phase])

    def coarse_finish(phase):
        wait_bytes(pk_r.at[phase, pl.ds(0, 15)], pk_rs.at[phase])
        everything = jnp.concatenate([pk_r[phase, q] for q in range(RING)], axis=1)
        picked = dot(everything, table[...]).astype(BF16)
        return weight[...] * (local[...] + dot(picked, basis_rows[...]))

    def grams(phase, z, others):
        z_hi, z_lo = split(z)
        highs, lows, at = [], [], 0
        for start, v in others:
            if start > at:
                highs.append(jnp.zeros((start - at, IFACE), BF16))
                lows.append(jnp.zeros((start - at, IFACE), BF16))
            hi, lo = split(v)
            highs.append(hi)
            lows.append(lo)
            at = start + CASES
        highs.append(jnp.zeros((LANES - at, IFACE), BF16))
        lows.append(jnp.zeros((LANES - at, IFACE), BF16))
        one = dot_nt(jnp.concatenate([z_hi, z_lo], axis=0), jnp.concatenate(highs, axis=0))
        two = dot_nt(z_hi, jnp.concatenate(lows, axis=0))
        mine = fold(one[0:CASES] + one[CASES:] + two)
        gram_s[phase] = mine
        gram_r[phase, pl.ds(yz, 1)] = mine[None]
        to_peers(lambda q: gram_s.at[phase], gram_r.at[phase, yz], gram_ss.at[phase], gram_rs.at[phase])

    def grams_layer(phase):
        wait_bytes(gram_r.at[phase, pl.ds(0, 15)], gram_rs.at[phase])
        return sum(gram_r[phase, q] for q in range(1, RING)) + gram_r[phase, 0]

    exchange_start(0, loads[...].astype(BF16))
    pcol_s_ref = pidx_s
    to_columns(pcol_s_ref, pidx_r.at[gx], px_ss.at[0], px_rs.at[0])
    pidx_r[pl.ds(gx, 1)] = pidx_s[...][None]
    loading[0].wait()
    chosen = jnp.where(iota((COARSE, LANES), 0) == prow, 1.0, 0.0).astype(BF16)
    inverse_cols = dot(cinv[...], chosen).astype(BF16)
    loading[1].wait()

    res = loads[...] + exchange_finish(0)
    weighted = weight[...] * res
    mine = coarse_terms(weighted)
    col_s[0, 0] = mine
    col_r[0, pl.ds(gx, 1), 0] = mine[None]
    columns_start(0, 1)
    wait_bytes(pidx_r.at[pl.ds(0, 15)], px_rs.at[0])
    owners = pack([pidx_r[g] for g in range(RING)])[0:8]
    pcol_s[...] = owners
    pcol_r[pl.ds(yz, 1)] = owners[None]
    to_peers(lambda q: pcol_s, pcol_r.at[yz], px_ss.at[1], px_rs.at[1])
    local[...] = dot(weighted.astype(BF16), linv[...])
    res_out[...] = res
    columns_wait(0, 1)
    packed = pack([col_r[0, g, 0] for g in range(RING)])
    packed_start(0, packed)
    terms0[...] = packed

    wait_bytes(pcol_r.at[pl.ds(0, 15)], px_rs.at[1])
    coarse_lane = iota((PACKED, COARSE), 1).astype(F32)

    def fill(p, carry):
        owner = jnp.transpose(pcol_r[p])
        one_hot = jnp.where(owner[:, 0:1] == coarse_lane, 1.0, 0.0).astype(BF16)
        table[pl.ds(pl.multiple_of(p * PACKED, PACKED), PACKED), :] = dot(one_hot, inverse_cols).astype(BF16)
        return carry

    lax.fori_loop(0, RING, fill, 0)

    t = coarse_finish(0)
    exchange_start(1, t.astype(BF16))
    loading[2].wait()
    z = t + exchange_finish(1)

    image = dot(z.astype(BF16), stiff[...])
    exchange_start(2, image.astype(BF16))
    grams(0, z, [(32, image), (48, weighted)])
    image = image + exchange_finish(2)
    mine = coarse_terms(weight[...] * image)
    layer = grams_layer(0)
    mine = jnp.where((lane8 % 64) < 32, mine, layer)
    col_s[1, 0] = mine
    col_r[1, pl.ds(gx, 1), 0] = mine[None]
    columns_start(1, 1)
    columns_wait(1, 1)
    tiles = [col_r[1, g, 0] for g in range(RING)]
    first = unfold(sum(tiles[1:]) + tiles[0])
    alpha = factor_t(eliminate(first, 32), 48)
    image_terms = pack(tiles)
    packed = terms0[...] - apply_t(alpha, image_terms)
    packed_start(1, packed)
    terms0[...] = packed
    res = res_out[...] - apply_t(alpha, image)
    weighted = weight[...] * res
    local[...] = dot(weighted.astype(BF16), linv[...])
    res_out[...] = res
    sol_out[...] = apply_t(alpha, z)
    pre_out[...] = z
    img[...] = image
    lane16 = iota((CASES, LANES), 1)
    identity = jnp.where(lane16 - 64 == iota((CASES, LANES), 0), 1.0, 0.0)
    inverse = lanes_of(eliminate(lanes_of(first, 48) + identity, 48), 64)
    t = coarse_finish(1)
    exchange_start(3, t.astype(BF16))
    z = t + exchange_finish(3)

    image = dot(z.astype(BF16), stiff[...])
    exchange_start(4, image.astype(BF16))
    grams(1, z, [(0, weight[...] * img[...]), (32, image), (48, weight[...] * res_out[...])])
    image = image + exchange_finish(4)
    mine = coarse_terms(weight[...] * image)
    layer = grams_layer(1)
    mine = jnp.where((lane8 % 64) < 32, mine, layer)
    col_s[2, 0] = mine
    col_s[2, 1] = layer
    col_r[2, pl.ds(gx, 1), 0] = mine[None]
    col_r[2, pl.ds(gx, 1), 1] = layer[None]
    columns_start(2, 2)
    columns_wait(2, 2)
    tiles = [col_r[2, g, 0] for g in range(RING)]
    second = unfold(sum(tiles[1:]) + tiles[0])
    cross = [col_r[2, g, 1] for g in range(RING)]
    cross = unfold(sum(cross[1:]) + cross[0])
    cross = jnp.concatenate([jnp.zeros((48, LANES), F32), cross, jnp.zeros((64, LANES), F32)], axis=0)
    cross_t = jnp.transpose(cross)[0:CASES, :]
    beta = apply_t(factor_t(inverse, 64), second)
    beta_t = factor_t(beta, 48)
    curve = apply_t(beta_t, cross_t + apply_t(factor_t(first, 32), beta))
    curve = curve + apply_t(factor_t(cross_t, 48), beta) + pltpu.roll(second, 16, 1)
    system = jnp.where(lane16 < 64, curve, pltpu.roll(second, 16, 1))
    alpha = factor_t(eliminate(system, 48), 64)
    new_terms = pack(tiles) + apply_t(beta_t, image_terms)
    packed_start(2, terms0[...] - apply_t(alpha, new_terms))
    image = image + apply_t(beta_t, img[...])
    res = res_out[...] - apply_t(alpha, image)
    local[...] = dot((weight[...] * res).astype(BF16), linv[...])
    res_out[...] = res
    direction = z + apply_t(beta_t, pre_out[...])
    sol_out[...] = sol_out[...] + apply_t(alpha, direction)
    t = coarse_finish(2)
    exchange_start(5, t.astype(BF16))
    pre_out[...] = t + exchange_finish(5)

    for phase in range(6):
        wait_bytes(slot_r.at[phase, pl.ds(0, 15)], slot_ss.at[phase])
        wait_bytes(face_r.at[phase], face_ss.at[phase])
    for phase in range(2):
        wait_bytes(gram_r.at[phase, pl.ds(0, 15)], gram_ss.at[phase])
    for phase in range(3):
        count = 2 if phase == 2 else 1
        wait_bytes(col_r.at[phase, pl.ds(0, 15), pl.ds(0, count)], col_ss.at[phase])
        wait_bytes(pk_r.at[phase, pl.ds(0, 15)], pk_ss.at[phase])
    wait_bytes(pidx_r.at[pl.ds(0, 15)], px_ss.at[0])
    wait_bytes(pcol_r.at[pl.ds(0, 15)], px_ss.at[1])


def per_device(*args):
    vector = jax.ShapeDtypeStruct((CASES, IFACE), F32)
    vmem = pl.BlockSpec(memory_space=pltpu.VMEM)
    hbm = pl.BlockSpec(memory_space=pl.ANY)
    dma = pltpu.SemaphoreType.DMA
    return pl.pallas_call(
        kernel,
        out_shape=(vector, vector, vector),
        in_specs=[vmem, hbm, hbm, vmem, hbm, vmem, vmem, vmem, vmem, vmem],
        out_specs=(vmem, vmem, vmem),
        scratch_shapes=[
            pltpu.VMEM((IFACE, IFACE), BF16),
            pltpu.VMEM((IFACE, IFACE), BF16),
            pltpu.VMEM((COARSE, COARSE), BF16),
            pltpu.VMEM((IFACE, NSLOT), BF16),
            pltpu.VMEM((NSLOT, IFACE), BF16),
            pltpu.VMEM((LANES, IFACE), BF16),
            pltpu.VMEM((IFACE, LANES), BF16),
            pltpu.VMEM((CASES, IFACE), F32),
            pltpu.VMEM((RING * PACKED, LANES), BF16),
            pltpu.VMEM((LANES, LANES), jnp.int32),
            pltpu.VMEM((24, LANES), jnp.int32),
            pltpu.VMEM((CASES, IFACE), F32),
            pltpu.VMEM((CASES, PACKED), F32),
            pltpu.VMEM((CASES, IFACE), F32),
            pltpu.VMEM((6, TILES, CASES, LANES), BF16),
            pltpu.VMEM((6, RING, CASES, LANES), BF16),
            pltpu.VMEM((6, 2, 2, CASES, LANES), BF16),
            pltpu.VMEM((2, 8, LANES), F32),
            pltpu.VMEM((2, RING, 8, LANES), F32),
            pltpu.VMEM((3, 2, 8, LANES), F32),
            pltpu.VMEM((3, RING, 2, 8, LANES), F32),
            pltpu.VMEM((3, CASES, PACKED), BF16),
            pltpu.VMEM((3, RING, CASES, PACKED), BF16),
            pltpu.VMEM((8, LANES), F32),
            pltpu.VMEM((RING, 8, LANES), F32),
            pltpu.VMEM((8, PACKED), F32),
            pltpu.VMEM((RING, 8, PACKED), F32),
            dma((3,)),
            dma((6,)), dma((6,)), dma((6,)), dma((6,)),
            dma((2,)), dma((2,)), dma((3,)), dma((3,)), dma((3,)), dma((3,)), dma((2,)), dma((2,)),
        ],
        compiler_params=pltpu.CompilerParams(
            collective_id=0, has_side_effects=True, vmem_limit_bytes=56 * 2**20
        ),
    )(*args)


def solution(mesh):
    whole = ("gx", "yz")
    columns, rows = P(None, whole), P(whole, None)
    lists = P(whole, None, None)
    return jax.shard_map(
        per_device,
        mesh=mesh,
        in_specs=(columns, rows, rows, columns, P(), rows, rows, lists, rows, lists),
        out_specs=(columns, columns, columns),
        check_vma=False,
    )
```

time: 829 us -> 96.3 us (0.12); the launches traced: 816 us -> 96 us
  blocking collectives: 500 us -> 0 us
  other arithmetic: 122 us -> 0 us
  Pallas kernels: 0 us -> 90.8 us
  local copies, waits for them, and re-layouts: 83 us -> 4.56 us
  starting transfers between devices: 60.3 us -> 0 us
  matrix products: 28.6 us -> 0 us
  waiting for transfers between devices: 20.1 us -> 0 us
    psum x6 -> x0, blocking collectives: 448 us -> none  [the longest x3 226 us: precondition(): coarse_total = lax.psum(spread, ('gx', 'yz'))]
    scatter-add x20 -> x0, other arithmetic: 96.3 us -> none  [the longest x6 47.4 us: assemble(): vector.at[:, across_list.reshape(-1)].add(arrived.reshape(cases, -1))]
    pallas_call x0 -> x1, Pallas kernels: none -> 90.8 us  [per_device(): pl.pallas_call(kernel, out_shape=(vector, vector, vector), in_specs=[vmem...]
    all_gather x3 -> x0, blocking collectives: 52 us -> none  [precondition(): coarse_solution = lax.all_gather(own_rows, 'gx', axis=1, tiled=True)]
    gather x21 -> x0, local copies, waits for them, and re-layouts: 46.4 us -> none  [the longest x12 27.3 us: assemble(): sending = jnp.take(vector, across_list, axis=1) * across_mask[None]]
    ppermute x12 -> x0, starting transfers between devices: 35.2 us -> none  [the longest x6 17.7 us: extended(): before = lax.ppermute(last, axis, up)]
    dot_general x26 -> x0, matrix products: 26.3 us -> none  [the longest x2 4.48 us: per_device(): jnp.dot(direction.astype(jnp.bfloat16), stiffness, preferred_element_type...]
    all_to_all x6 -> x0, starting transfers between devices: 25.1 us -> none  [assemble(): lax.all_to_all(sending.astype(jnp.bfloat16), 'yz', split_axis=1, concat_a...]
  transfers between devices with their start and end apart: 18 -> 0, of which waited for: 4 -> 0; matrix products, arithmetic and copies ran while one was open for 14% -> 0% of each run, Pallas kernels for 0% -> 0%
where the time goes in v1:
time: 96.3 us; the launch traced here: 96 us
  Pallas kernels  90.8 us (94%)
  local copies, waits for them, and re-layouts  4.56 us (5%)
    pallas_call x1, Pallas kernels, per_device(): pl.pallas_call(kernel, out_shape=(vector, vector, vector), in_specs=[vmem...  90.8 us
    unnamed x3, local copies, waits for them, and re-layouts  4.56 us

profile of v1, /device:TPU:1, one launch (start us, length us, event | category | flops | bytes accessed | tf_op | source)
XLA Modules:
  0.0 96.0 jit_solution(1258653883758737589)
XLA Ops:
  0.6 90.8 %shard_map.121 = (f32[16,1152]{1,0:T(8,128)}, f32[16,1152]{1,0:T(8,128)}, f32[16,1152]{1,0:T(8,128)}) custom-call(f32[16,1152]{1,0:T(8,128)} %loads.1, bf16[1152,1152]{1,0:T(8,128)(2,1)} %stiff_hbm.1, bf16[1152,1152]{1,0:T(8,128)(2,1)} %linv_hbm.1, bf16[24,1152]{1,0:T(8,128)(2,1)} %basis.1, bf16[1024,1024]{1,0:T(8,128)(2,1)} %cinv_hbm.1, s32[1,24]{1,0:T(1,128)} %primal.1, ...), custom_call_target="tpu_custom_call" | custom-call | tf_op jit(solution)/shard_map/pallas_call | solution.py:398
  91.5 1.5 %copy.16 = f32[16,1152]{1,0:T(8,128)} copy(f32[16,1152]{1,0:T(8,128)} %get-tuple-element.6) | data formatting | bytes 147456
  93.0 1.5 %copy.17 = f32[16,1152]{1,0:T(8,128)} copy(f32[16,1152]{1,0:T(8,128)} %get-tuple-element.7) | data formatting | bytes 147456
  94.5 1.5 %copy.18 = f32[16,1152]{1,0:T(8,128)} copy(f32[16,1152]{1,0:T(8,128)} %get-tuple-element.8) | data formatting | bytes 147456

commit v2 on v1

v2 whole, which is shorter than its diff:
```python
import functools

import jax
import jax.numpy as jnp
from jax import lax
from jax.experimental import pallas as pl
from jax.experimental.pallas import tpu as pltpu
from jax.sharding import PartitionSpec as P

MESH = pl.DeviceIdType.MESH
F32, BF16 = jnp.float32, jnp.bfloat16

CASES = 16
IFACE = 1152
PRIMAL = 24
SLOTS = 48
FACE = 144
COARSE = 1024
RING = 16
TILES = 11
LANES = 128
NSLOT = TILES * LANES
PACKED = 512
HALF = 512
BLOCK = 32
EXT = 640


def dot(a, b):
    return jnp.dot(a, b, preferred_element_type=F32)


def dot_nt(a, b):
    return lax.dot_general(a, b, (((1,), (1,)), ((), ())), preferred_element_type=F32)


def split(x):
    hi = x.astype(BF16)
    return hi, (x - hi.astype(F32)).astype(BF16)


def iota(shape, dim):
    return lax.broadcasted_iota(jnp.int32, shape, dim)


def fold(m):
    lane = iota((8, LANES), 1)
    return jnp.where(lane < 64, m[0:8], pltpu.roll(m[8:16], 64, 1))


def unfold(m):
    return jnp.concatenate([m, pltpu.roll(m, 64, 1)], axis=0)


def pack(tiles):
    lane = iota((8, LANES), 1)
    keep = (lane % 64) < 32
    pairs = []
    for i in range(8):
        even = jnp.where(keep, tiles[2 * i], 0.0)
        odd = jnp.where(keep, tiles[2 * i + 1], 0.0)
        pairs.append(even + pltpu.roll(odd, 32, 1))
    columns = []
    for i in range(4):
        a, b = pairs[2 * i], pairs[2 * i + 1]
        top = jnp.where(lane < 64, a, pltpu.roll(b, 64, 1))
        low = jnp.where(lane < 64, pltpu.roll(a, 64, 1), b)
        columns.append(jnp.concatenate([top, low], axis=0))
    return jnp.concatenate(columns, axis=1)


def eliminate(m, base):
    rows = iota((CASES, LANES), 0)
    for k in range(CASES):
        row = m[k : k + 1, :]
        scaled = row * (1.0 / row[:, base + k : base + k + 1])
        m = jnp.where(rows == k, scaled, m - m[:, base + k : base + k + 1] * scaled)
    return m


def lanes_of(m, start):
    lane = iota(m.shape, 1)
    return jnp.where((lane >= start) & (lane < start + CASES), m, 0.0)


def split3(x):
    a = x.astype(BF16)
    rest = x - a.astype(F32)
    b = rest.astype(BF16)
    return a, b, (rest - b.astype(F32)).astype(BF16)


def factor_t(m, start):
    a, b, c = (part.astype(F32) for part in split3(m))
    stack = jnp.concatenate([a, a, a, b, b, c, jnp.zeros((LANES - 6 * CASES, LANES), F32)], axis=0)
    return jnp.transpose(stack)[start : start + CASES, :].astype(BF16)


def apply_t(left, v):
    a, b, c = split3(v)
    pad = jnp.zeros((LANES - 6 * CASES, v.shape[1]), BF16)
    return dot(left, jnp.concatenate([a, b, c, a, b, a, pad], axis=0))


def kernel(
    loads, stiff_hbm, linv_hbm, basis, cinv_hbm, primal, lcounts, lindex, acounts, aindex,
    sol_out, res_out, pre_out,
    stiff, linv, cinv, gather, scatter, basis_cols, weight, spread, near, near_inverse,
    idx, lidx, smooth, terms0, img, img_smooth,
    slot_s, slot_r, face_r, wide_s, wide_r, wface_r, gram_s, gram_r, col_s, col_r,
    half_s, half_r, sib_s, sib_r, pidx_s, pidx_rp, pidx_rc,
    load_sem, slot_ss, slot_rs, face_ss, face_rs, wide_ss, wide_rs, wface_ss, wface_rs,
    gram_ss, gram_rs, col_ss, col_rs, half_ss, half_rs, sib_ss, sib_rs, px_ss, px_rs,
):
    gx, yz = lax.axis_index("gx"), lax.axis_index("yz")
    y, x = yz // 4, yz % 4
    offsets = sorted(
        [(a, b) for a in range(4) for b in range(4) if (a, b) != (0, 0)],
        key=lambda o: -(min(o[0], 4 - o[0]) + min(o[1], 4 - o[1])),
    )
    peers = [((y + a) % 4) * 4 + (x + b) % 4 for a, b in offsets]
    zs = sorted(range(1, RING), key=lambda o: -min(o, RING - o))
    columns = [(gx + o) % RING for o in zs]
    below, above = (gx + RING - 1) % RING, (gx + 1) % RING
    core = gx % 2
    sibling = gx + 1 - 2 * core

    barrier = pltpu.get_barrier_semaphore()
    for q in peers:
        pl.semaphore_signal(barrier, 1, device_id=(gx, q), device_id_type=MESH)
    for q in columns:
        pl.semaphore_signal(barrier, 1, device_id=(q, yz), device_id_type=MESH)

    loading = [
        pltpu.make_async_copy(linv_hbm, linv, load_sem.at[0]),
        pltpu.make_async_copy(cinv_hbm, cinv, load_sem.at[1]),
        pltpu.make_async_copy(stiff_hbm, stiff, load_sem.at[2]),
    ]
    for copy in loading:
        copy.start()

    sent = []

    def wait_bytes(ref, sem):
        pltpu.make_async_copy(ref, ref, sem).wait()

    def send(src, dst, ssem, rsem, device):
        pltpu.make_async_remote_copy(src, dst, ssem, rsem, device_id=device, device_id_type=MESH).start()

    def to_peers(src, dst, arrivals, ssem, rsem):
        for q in peers:
            send(src(q), dst, ssem, rsem, (gx, q))
        sent.append((arrivals, ssem))

    def to_columns(src, dst, arrivals, ssem, rsem):
        for q in columns:
            send(src, dst, ssem, rsem, (q, yz))
        sent.append((arrivals, ssem))

    lane1 = iota((1, LANES), 1)
    lane8 = iota((8, LANES), 1)
    lane16 = iota((CASES, LANES), 1)
    idx[...] = jnp.full((LANES, LANES), -1, jnp.int32)
    lidx[...] = jnp.full((24, LANES), -1, jnp.int32)
    slot_lane = iota((1, SLOTS), 1)
    for q in range(RING):
        lidx[q : q + 1, 0:SLOTS] = jnp.where(slot_lane < acounts[0:1, q : q + 1], aindex[0, q : q + 1, :], -1)
    idx[0:8, :] = jnp.where(lane8 < 64, lidx[0:8, :], pltpu.roll(lidx[8:16, :], 64, 1))
    face_lane = iota((1, FACE), 1)
    low = jnp.where(face_lane < lcounts[0:1, 0:1], lindex[0, 0:1, :], -1)
    up = jnp.where(face_lane < lcounts[0:1, 1:2], lindex[0, 1:2, :], -1)
    lidx[16:17, 0 : FACE - LANES] = low[:, LANES:FACE]
    lidx[17:18, 0 : FACE - LANES] = up[:, LANES:FACE]
    idx[8:9, :] = low[:, 0:LANES]
    idx[9:10, :] = jnp.where(lane1 < 64, lidx[16:17, :], pltpu.roll(lidx[17:18, :], 64, 1))
    idx[10:11, :] = up[:, 0:LANES]
    lidx[18:19, 0:PRIMAL] = primal[...]
    row_iota = iota((IFACE, LANES), 0)
    for b in range(TILES):
        gather[:, b * LANES : (b + 1) * LANES] = jnp.where(row_iota == idx[b : b + 1, :], 1.0, 0.0).astype(BF16)

    def exchange_values(sends, phase, values):
        out = dot(values, gather[...]).astype(BF16)
        for b in range(TILES):
            sends[phase, b] = out[:, b * LANES : (b + 1) * LANES]

    def exchange_send(phase, sends, arrived, faces, ss, rs, fss, frs):
        to_peers(
            lambda q: sends.at[phase, q % 8], arrived.at[phase, yz], arrived.at[phase, pl.ds(0, 15)],
            ss.at[phase], rs.at[phase],
        )
        send(sends.at[phase, pl.ds(8, 2)], faces.at[phase, 1], fss.at[phase], frs.at[phase], (below, yz))
        send(sends.at[phase, pl.ds(9, 2)], faces.at[phase, 0], fss.at[phase], frs.at[phase], (above, yz))
        sent.append((faces.at[phase], fss.at[phase]))

    def exchange_arrived(phase, arrived, faces, rs, frs):
        wait_bytes(faces.at[phase], frs.at[phase])
        wait_bytes(arrived.at[phase, pl.ds(0, 15)], rs.at[phase])
        lane = iota(arrived.shape[2:], 1)
        first = yz < 8
        mine = (lane < 64) == first
        parts = []
        for b in range(8):
            a, c = arrived[phase, b].astype(F32), arrived[phase, b + 8].astype(F32)
            stay = jnp.where(first, a, c)
            move = jnp.where(first, c, a)
            parts.append(jnp.where(mine, stay, pltpu.roll(move, 64, 1)))
        parts.append(faces[phase, 0, 1].astype(F32))
        tails = jnp.where(lane < 64, faces[phase, 1, 1].astype(F32), faces[phase, 0, 0].astype(F32))
        parts.append(pltpu.roll(tails, 64, 1))
        parts.append(faces[phase, 1, 0].astype(F32))
        return parts

    def exchange_start(phase, values):
        exchange_values(slot_s, phase, values)
        exchange_send(phase, slot_s, slot_r, face_r, slot_ss, slot_rs, face_ss, face_rs)

    def exchange_finish(phase):
        parts = exchange_arrived(phase, slot_r, face_r, slot_rs, face_rs)
        return dot(jnp.concatenate(parts, axis=1).astype(BF16), scatter[...])

    def wide_start(phase, values):
        exchange_values(wide_s, phase, values)
        exchange_send(phase, wide_s, wide_r, wface_r, wide_ss, wide_rs, wface_ss, wface_rs)

    def smooth_start(phase, weighted):
        hi, lo = split(weighted)
        both = dot(jnp.concatenate([hi, lo], axis=0), linv[...])
        part = weight[...] * (both[0:CASES] + both[CASES:])
        hi, lo = split(part)
        wide_start(phase, jnp.concatenate([hi, lo], axis=0))
        return part

    def smooth_finish(phase):
        parts = exchange_arrived(phase, wide_r, wface_r, wide_rs, wface_rs)
        both = dot(jnp.concatenate(parts, axis=1).astype(BF16), scatter[...])
        return both[0:CASES] + both[CASES:]

    def coarse_terms(weighted):
        hi, lo = split(weighted)
        both = dot(jnp.concatenate([hi, lo], axis=0), basis_cols[...])
        return fold(both[0:CASES] + both[CASES:])

    def columns_start(phase, count):
        to_columns(
            col_s.at[phase, pl.ds(0, count)], col_r.at[phase, gx, pl.ds(0, count)],
            col_r.at[phase, pl.ds(0, 15), pl.ds(0, count)], col_ss.at[phase], col_rs.at[phase],
        )

    def columns_wait(phase, count):
        wait_bytes(col_r.at[phase, pl.ds(0, 15), pl.ds(0, count)], col_rs.at[phase])

    def coarse_start(phase, packed):
        hi, lo = split(packed)
        both = dot(jnp.concatenate([hi, lo], axis=0), spread[...])
        out = (both[0:CASES] + both[CASES:]).astype(BF16)
        half_s[phase] = out
        half_r[phase, pl.ds(yz, 1)] = out[None]
        arrivals = half_r.at[phase, pl.ds(0, 15)]
        to_peers(lambda q: half_s.at[phase], half_r.at[phase, yz], arrivals, half_ss.at[phase], half_rs.at[phase])

    def coarse_finish(phase):
        wait_bytes(half_r.at[phase, pl.ds(0, 15)], half_rs.at[phase])
        total = half_r[phase, 0].astype(F32)
        for q in range(1, RING):
            total = total + half_r[phase, q].astype(F32)
        sib_s[phase] = total
        send(sib_s.at[phase], sib_r.at[phase], sib_ss.at[phase], sib_rs.at[phase], (sibling, yz))
        sent.append((sib_s.at[phase], sib_ss.at[phase]))
        own = pl.ds(pl.multiple_of(core * HALF, HALF), HALF)
        other = pl.ds(pl.multiple_of((1 - core) * HALF, HALF), HALF)
        picked = dot(total.astype(BF16), near_inverse[own, :])
        wait_bytes(sib_r.at[phase], sib_rs.at[phase])
        picked = picked + dot(sib_r[phase].astype(BF16), near_inverse[other, :])
        return dot(picked.astype(BF16), near[...])

    def grams(phase, z, others):
        z_hi, z_lo = split(z)
        highs, lows, at = [], [], 0
        for start, v in others:
            if start > at:
                highs.append(jnp.zeros((start - at, IFACE), BF16))
                lows.append(jnp.zeros((start - at, IFACE), BF16))
            hi, lo = split(v)
            highs.append(hi)
            lows.append(lo)
            at = start + CASES
        highs.append(jnp.zeros((LANES - at, IFACE), BF16))
        lows.append(jnp.zeros((LANES - at, IFACE), BF16))
        one = dot_nt(jnp.concatenate([z_hi, z_lo], axis=0), jnp.concatenate(highs, axis=0))
        two = dot_nt(z_hi, jnp.concatenate(lows, axis=0))
        mine = fold(one[0:CASES] + one[CASES:] + two)
        gram_s[phase] = mine
        gram_r[phase, pl.ds(yz, 1)] = mine[None]
        arrivals = gram_r.at[phase, pl.ds(0, 15)]
        to_peers(lambda q: gram_s.at[phase], gram_r.at[phase, yz], arrivals, gram_ss.at[phase], gram_rs.at[phase])

    def grams_layer(phase):
        wait_bytes(gram_r.at[phase, pl.ds(0, 15)], gram_rs.at[phase])
        return sum(gram_r[phase, q] for q in range(1, RING)) + gram_r[phase, 0]

    for phase in range(3):
        slot_r[phase, pl.ds(yz, 1)] = jnp.zeros((1, CASES, LANES), BF16)
    for phase in range(4):
        wide_r[phase, pl.ds(yz, 1)] = jnp.zeros((1, BLOCK, LANES), BF16)
    prow8 = jnp.broadcast_to(lidx[18:19, :].astype(F32), (8, LANES))
    primals = jnp.where(lane8 < 32, prow8, jnp.where((lane8 >= 64) & (lane8 < 96), pltpu.roll(prow8, 64, 1), 0.0))
    pidx_s[...] = primals
    pidx_rp[pl.ds(yz, 1)] = primals[None]
    pidx_rc[pl.ds(gx, 1)] = primals[None]
    exchange_values(slot_s, 0, loads[...].astype(BF16))

    pl.semaphore_wait(barrier, len(peers) + len(columns))

    exchange_send(0, slot_s, slot_r, face_r, slot_ss, slot_rs, face_ss, face_rs)
    to_columns(pidx_s, pidx_rc.at[gx], pidx_rc.at[pl.ds(0, 15)], px_ss.at[0], px_rs.at[0])
    to_peers(lambda q: pidx_s, pidx_rp.at[yz], pidx_rp.at[pl.ds(0, 15)], px_ss.at[1], px_rs.at[1])
    idx_cols = jnp.transpose(idx[...].astype(F32))
    lane_iota = iota((LANES, IFACE), 1).astype(F32)
    for b in range(TILES):
        scatter[b * LANES : (b + 1) * LANES, :] = jnp.where(idx_cols[:, b : b + 1] == lane_iota, 1.0, 0.0).astype(BF16)
    weight[...] = 1.0 / (1.0 + dot(jnp.ones((CASES, NSLOT), BF16), scatter[...]))
    basis_f32 = basis[...].astype(F32)
    basis_pad = jnp.concatenate([basis_f32, jnp.zeros((LANES - PRIMAL, IFACE), F32)], axis=0)
    basis_cols[...] = jnp.transpose(basis_pad).astype(BF16)
    scaled = jnp.concatenate([weight[...] * basis_pad[0:CASES], weight[...] * basis_pad[CASES:BLOCK]], axis=0)
    scaled = scaled.astype(BF16)
    wide_start(3, scaled)
    loading[0].wait()

    res = loads[...] + exchange_finish(0)
    weighted = weight[...] * res
    mine = coarse_terms(weighted)
    col_s[0, 0] = mine
    col_r[0, pl.ds(gx, 1), 0] = mine[None]
    columns_start(0, 1)
    own_smooth = smooth_start(0, weighted)
    res_out[...] = res

    wait_bytes(pidx_rc.at[pl.ds(0, 15)], px_rs.at[0])
    owners = jnp.transpose(pack([pidx_rc[g] for g in range(RING)])[0:8])
    half_lane = (iota((PACKED, HALF), 1) + core * HALF).astype(F32)
    spread[...] = jnp.where(owners[:, 0:1] == half_lane, 1.0, 0.0).astype(BF16)
    columns_wait(0, 1)
    packed = pack([col_r[0, g, 0] for g in range(RING)])
    coarse_start(0, packed)
    terms0[...] = packed

    wait_bytes(pidx_rp.at[pl.ds(0, 15)], px_rs.at[1])
    across_primals = pack([pidx_rp[q] for q in range(RING)])[0:8]
    lower = pidx_rc[pl.ds(below, 1)][0]
    upper = pltpu.roll(pidx_rc[pl.ds(above, 1)][0], 32, 1)
    face_primals = jnp.where(lane8 < 32, lower, jnp.where(lane8 < 64, upper, -1.0))
    near_row = jnp.concatenate([across_primals, face_primals], axis=1)[0:1]
    chosen = jnp.where(iota((COARSE, EXT), 0).astype(F32) == near_row, 1.0, 0.0).astype(BF16)
    loading[1].wait()
    near_inverse[...] = dot(cinv[...], chosen).astype(BF16)

    parts = exchange_arrived(3, wide_r, wface_r, wide_rs, wface_rs)
    lane32 = iota((BLOCK, LANES), 1)
    for b in range(8):
        both = jnp.concatenate([jnp.where(lane32 < 64, parts[b], 0.0), jnp.where(lane32 < 64, 0.0, parts[b])], axis=0)
        rows = dot(both.astype(BF16), scatter[b * LANES : (b + 1) * LANES, :]).astype(BF16)
        near[b * BLOCK : (b + 1) * BLOCK, :] = rows[0:BLOCK]
        near[(b + 8) * BLOCK : (b + 9) * BLOCK, :] = rows[BLOCK:]
    none = jnp.zeros((BLOCK, LANES), F32)
    faces = jnp.concatenate([
        jnp.concatenate([parts[8], jnp.where(lane32 < 64, parts[9], 0.0), none], axis=1),
        jnp.concatenate([none, jnp.where(lane32 < 64, 0.0, parts[9]), parts[10]], axis=1),
    ], axis=0)
    near[16 * BLOCK : 18 * BLOCK, :] = dot(faces.astype(BF16), scatter[8 * LANES :, :]).astype(BF16)
    near[18 * BLOCK :, :] = jnp.zeros((EXT - 18 * BLOCK, IFACE), BF16)
    near[pl.ds(pl.multiple_of(yz * BLOCK, BLOCK), BLOCK), :] = scaled

    own_smooth = own_smooth + smooth_finish(0)
    smooth[...] = own_smooth
    loading[2].wait()
    z = own_smooth + coarse_finish(0)

    image = dot(z.astype(BF16), stiff[...])
    exchange_start(1, image.astype(BF16))
    grams(0, z, [(32, image), (48, weighted)])
    image = image + exchange_finish(1)
    weighted = weight[...] * image
    mine = coarse_terms(weighted)
    mine = jnp.where((lane8 % 64) < 32, mine, grams_layer(0))
    col_s[1, 0] = mine
    col_r[1, pl.ds(gx, 1), 0] = mine[None]
    columns_start(1, 1)
    own_smooth = smooth_start(1, weighted)
    img[...] = image
    columns_wait(1, 1)
    tiles = [col_r[1, g, 0] for g in range(RING)]
    first = unfold(sum(tiles[1:]) + tiles[0])
    image_terms = pack(tiles)
    alpha = factor_t(eliminate(first, 32), 48)
    packed = terms0[...] - apply_t(alpha, image_terms)
    coarse_start(1, packed)
    terms0[...] = packed
    res_out[...] = res_out[...] - apply_t(alpha, image)
    sol_out[...] = apply_t(alpha, z)
    pre_out[...] = z
    identity = jnp.where(lane16 - 64 == iota((CASES, LANES), 0), 1.0, 0.0)
    inverse = eliminate(lanes_of(first, 48) + identity, 48)
    own_smooth = own_smooth + smooth_finish(1)
    img_smooth[...] = own_smooth
    own_smooth = smooth[...] - apply_t(alpha, own_smooth)
    smooth[...] = own_smooth
    z = own_smooth + coarse_finish(1)

    image = dot(z.astype(BF16), stiff[...])
    exchange_start(2, image.astype(BF16))
    grams(1, z, [(0, weight[...] * img[...]), (32, image), (48, weight[...] * res_out[...])])
    image = image + exchange_finish(2)
    weighted = weight[...] * image
    mine = coarse_terms(weighted)
    layer = grams_layer(1)
    mine = jnp.where((lane8 % 64) < 32, mine, layer)
    col_s[2, 0] = mine
    col_s[2, 1] = layer
    col_r[2, pl.ds(gx, 1), 0] = mine[None]
    col_r[2, pl.ds(gx, 1), 1] = layer[None]
    columns_start(2, 2)
    own_smooth = smooth_start(2, weighted)
    columns_wait(2, 2)
    tiles = [col_r[2, g, 0] for g in range(RING)]
    second = unfold(sum(tiles[1:]) + tiles[0])
    cross = [col_r[2, g, 1] for g in range(RING)]
    cross = unfold(sum(cross[1:]) + cross[0])
    cross = jnp.concatenate([jnp.zeros((48, LANES), F32), cross, jnp.zeros((64, LANES), F32)], axis=0)
    cross_t = jnp.transpose(cross)[0:CASES, :]
    beta = apply_t(factor_t(inverse, 64), second)
    beta_t = factor_t(beta, 48)
    curve = apply_t(beta_t, cross_t + apply_t(factor_t(first, 32), beta))
    curve = curve + apply_t(factor_t(cross_t, 48), beta) + pltpu.roll(second, 16, 1)
    system = jnp.where(lane16 < 64, curve, pltpu.roll(second, 16, 1))
    new_terms = pack(tiles) + apply_t(beta_t, image_terms)
    alpha = factor_t(eliminate(system, 48), 64)
    coarse_start(2, terms0[...] - apply_t(alpha, new_terms))
    image = image + apply_t(beta_t, img[...])
    res_out[...] = res_out[...] - apply_t(alpha, image)
    direction = z + apply_t(beta_t, pre_out[...])
    sol_out[...] = sol_out[...] + apply_t(alpha, direction)
    own_smooth = own_smooth + smooth_finish(2) + apply_t(beta_t, img_smooth[...])
    own_smooth = smooth[...] - apply_t(alpha, own_smooth)
    pre_out[...] = own_smooth + coarse_finish(2)

    for arrivals, ssem in sent:
        wait_bytes(arrivals, ssem)


def hand_over(a, b, c, a_out, b_out, c_out, sems):
    copies = [
        pltpu.make_async_copy(src, dst, sems.at[i])
        for i, (src, dst) in enumerate([(a, a_out), (b, b_out), (c, c_out)])
    ]
    for copy in copies:
        copy.start()
    for copy in copies:
        copy.wait()


def per_device(*args):
    vector = jax.ShapeDtypeStruct((CASES, IFACE), F32)
    vmem = pl.BlockSpec(memory_space=pltpu.VMEM)
    hbm = pl.BlockSpec(memory_space=pl.ANY)
    dma = pltpu.SemaphoreType.DMA
    results = pl.pallas_call(
        kernel,
        out_shape=(vector, vector, vector),
        in_specs=[vmem, hbm, hbm, vmem, hbm, vmem, vmem, vmem, vmem, vmem],
        out_specs=(vmem, vmem, vmem),
        scratch_shapes=[
            pltpu.VMEM((IFACE, IFACE), BF16),
            pltpu.VMEM((IFACE, IFACE), BF16),
            pltpu.VMEM((COARSE, COARSE), BF16),
            pltpu.VMEM((IFACE, NSLOT), BF16),
            pltpu.VMEM((NSLOT, IFACE), BF16),
            pltpu.VMEM((IFACE, LANES), BF16),
            pltpu.VMEM((CASES, IFACE), F32),
            pltpu.VMEM((PACKED, HALF), BF16),
            pltpu.VMEM((EXT, IFACE), BF16),
            pltpu.VMEM((COARSE, EXT), BF16),
            pltpu.VMEM((LANES, LANES), jnp.int32),
            pltpu.VMEM((24, LANES), jnp.int32),
            pltpu.VMEM((CASES, IFACE), F32),
            pltpu.VMEM((CASES, PACKED), F32),
            pltpu.VMEM((CASES, IFACE), F32),
            pltpu.VMEM((CASES, IFACE), F32),
            pltpu.VMEM((3, TILES, CASES, LANES), BF16),
            pltpu.VMEM((3, RING, CASES, LANES), BF16),
            pltpu.VMEM((3, 2, 2, CASES, LANES), BF16),
            pltpu.VMEM((4, TILES, BLOCK, LANES), BF16),
            pltpu.VMEM((4, RING, BLOCK, LANES), BF16),
            pltpu.VMEM((4, 2, 2, BLOCK, LANES), BF16),
            pltpu.VMEM((2, 8, LANES), F32),
            pltpu.VMEM((2, RING, 8, LANES), F32),
            pltpu.VMEM((3, 2, 8, LANES), F32),
            pltpu.VMEM((3, RING, 2, 8, LANES), F32),
            pltpu.VMEM((3, CASES, HALF), BF16),
            pltpu.VMEM((3, RING, CASES, HALF), BF16),
            pltpu.VMEM((3, CASES, HALF), F32),
            pltpu.VMEM((3, CASES, HALF), F32),
            pltpu.VMEM((8, LANES), F32),
            pltpu.VMEM((RING, 8, LANES), F32),
            pltpu.VMEM((RING, 8, LANES), F32),
            dma((3,)),
            dma((3,)), dma((3,)), dma((3,)), dma((3,)),
            dma((4,)), dma((4,)), dma((4,)), dma((4,)),
            dma((2,)), dma((2,)), dma((3,)), dma((3,)),
            dma((3,)), dma((3,)), dma((3,)), dma((3,)), dma((2,)), dma((2,)),
        ],
        compiler_params=pltpu.CompilerParams(
            collective_id=0, has_side_effects=True, vmem_limit_bytes=56 * 2**20
        ),
    )(*args)
    return pl.pallas_call(
        hand_over,
        out_shape=(vector, vector, vector),
        in_specs=[hbm, hbm, hbm],
        out_specs=(hbm, hbm, hbm),
        scratch_shapes=[dma((3,))],
        compiler_params=pltpu.CompilerParams(vmem_limit_bytes=60 * 2**20),
    )(*results)


def solution(mesh):
    whole = ("gx", "yz")
    columns, rows = P(None, whole), P(whole, None)
    lists = P(whole, None, None)
    return jax.shard_map(
        per_device,
        mesh=mesh,
        in_specs=(columns, rows, rows, columns, P(), rows, rows, lists, rows, lists),
        out_specs=(columns, columns, columns),
        check_vma=False,
    )
```

time: 96.3 us -> 79.7 us (0.83)
  Pallas kernels: 90.8 us -> 78.8 us
  local copies, waits for them, and re-layouts: 4.56 us -> 0 us
    pallas_call x1, Pallas kernels: 90.8 us -> 71 us  [per_device(): pl.pallas_call(kernel, out_shape=(vector, vector, vector), in_specs=[vmem...]
    pallas_call x0 -> x1, Pallas kernels: none -> 7.83 us  [per_device(): pl.pallas_call(hand_over, out_shape=(vector, vector, vector), in_specs=[h...]
    unnamed x3 -> x0, local copies, waits for them, and re-layouts: 4.56 us -> none
where the time goes in v2:
time: 79.7 us; the launch traced here: 79.6 us
  Pallas kernels  78.8 us (99%)
  between operations  0.8 us (1%)
    pallas_call x1, Pallas kernels, per_device(): pl.pallas_call(kernel, out_shape=(vector, vector, vector), in_specs=[vmem...  71 us
    pallas_call x1, Pallas kernels, per_device(): pl.pallas_call(hand_over, out_shape=(vector, vector, vector), in_specs=[h...  7.83 us

profile of v2, /device:TPU:1, one launch (start us, length us, event | category | flops | bytes accessed | tf_op | source)
XLA Modules:
  0.0 79.6 jit_solution(3258337470045693230)
XLA Ops:
  0.6 71.0 %shard_map.121 = (f32[16,1152]{1,0:T(8,128)}, f32[16,1152]{1,0:T(8,128)}, f32[16,1152]{1,0:T(8,128)}) custom-call(f32[16,1152]{1,0:T(8,128)} %loads.1, bf16[1152,1152]{1,0:T(8,128)(2,1)} %stiff_hbm.1, bf16[1152,1152]{1,0:T(8,128)(2,1)} %linv_hbm.1, bf16[24,1152]{1,0:T(8,128)(2,1)} %basis.1, bf16[1024,1024]{1,0:T(8,128)(2,1)} %cinv_hbm.1, s32[1,24]{1,0:T(1,128)} %primal.1, ...), custom_call_target="tpu_custom_call" | custom-call | tf_op jit(solution)/shard_map/pallas_call | solution.py:468
  71.6 7.8 %shard_map.122 = (f32[16,1152]{1,0:T(8,128)}, f32[16,1152]{1,0:T(8,128)}, f32[16,1152]{1,0:T(8,128)}) custom-call(f32[16,1152]{1,0:T(8,128)} %get-tuple-element.6.a, f32[16,1152]{1,0:T(8,128)} %get-tuple-element.7.b, f32[16,1152]{1,0:T(8,128)} %get-tuple-element.8.c), custom_call_target="tpu_custom_call" | custom-call | tf_op jit(solution)/shard_map/pallas_call | solution.py:517

commit v3 on v2

--- a/solution.py
+++ b/solution.py
@@ -105,12 +105,12 @@
 def kernel(
     loads, stiff_hbm, linv_hbm, basis, cinv_hbm, primal, lcounts, lindex, acounts, aindex,
     sol_out, res_out, pre_out,
-    stiff, linv, cinv, gather, scatter, basis_cols, weight, spread, near, near_inverse,
-    idx, lidx, smooth, terms0, img, img_smooth,
-    slot_s, slot_r, face_r, wide_s, wide_r, wface_r, gram_s, gram_r, col_s, col_r,
-    half_s, half_r, sib_s, sib_r, pidx_s, pidx_rp, pidx_rc,
+    stiff, linv, cinv, gather, scatter, basis_cols, weight, spread, near, near_t, chosen_t, near_inverse,
+    idx, lidx, smooth, rhs, img, img_smooth, img_rhs,
+    slot_s, slot_r, face_r, wide_s, wide_r, wface_r, gram_s, gram_r, ring_s, ring_r, col_s, col_r,
+    half_s, half_r, sib_s, sib_r, part_s, part_r, sum_s, sum_r, all_s, all_r, pidx_s, pidx_rp, pidx_rc,
     load_sem, slot_ss, slot_rs, face_ss, face_rs, wide_ss, wide_rs, wface_ss, wface_rs,
-    gram_ss, gram_rs, col_ss, col_rs, half_ss, half_rs, sib_ss, sib_rs, px_ss, px_rs,
+    gram_ss, gram_rs, ring_ss, ring_rs, part_ss, part_rs, sum_ss, sum_rs, all_ss, all_rs, one_ss, one_rs,
 ):
     gx, yz = lax.axis_index("gx"), lax.axis_index("yz")
     y, x = yz // 4, yz % 4
@@ -241,37 +241,71 @@
         both = dot(jnp.concatenate([hi, lo], axis=0), basis_cols[...])
         return fold(both[0:CASES] + both[CASES:])
 
-    def columns_start(phase, count):
-        to_columns(
-            col_s.at[phase, pl.ds(0, count)], col_r.at[phase, gx, pl.ds(0, count)],
-            col_r.at[phase, pl.ds(0, 15), pl.ds(0, count)], col_ss.at[phase], col_rs.at[phase],
-        )
-
-    def columns_wait(phase, count):
-        wait_bytes(col_r.at[phase, pl.ds(0, 15), pl.ds(0, count)], col_rs.at[phase])
-
-    def coarse_start(phase, packed):
+    def coarse_start(packed):
         hi, lo = split(packed)
         both = dot(jnp.concatenate([hi, lo], axis=0), spread[...])
         out = (both[0:CASES] + both[CASES:]).astype(BF16)
-        half_s[phase] = out
-        half_r[phase, pl.ds(yz, 1)] = out[None]
-        arrivals = half_r.at[phase, pl.ds(0, 15)]
-        to_peers(lambda q: half_s.at[phase], half_r.at[phase, yz], arrivals, half_ss.at[phase], half_rs.at[phase])
-
-    def coarse_finish(phase):
-        wait_bytes(half_r.at[phase, pl.ds(0, 15)], half_rs.at[phase])
-        total = half_r[phase, 0].astype(F32)
+        half_s[...] = out
+        half_r[pl.ds(yz, 1)] = out[None]
+        to_peers(lambda q: half_s, half_r.at[yz], half_r.at[pl.ds(0, 15)], one_ss.at[1], one_rs.at[1])
+
+    def coarse_finish():
+        wait_bytes(half_r.at[pl.ds(0, 15)], one_rs.at[1])
+        total = half_r[0].astype(F32)
         for q in range(1, RING):
-            total = total + half_r[phase, q].astype(F32)
-        sib_s[phase] = total
-        send(sib_s.at[phase], sib_r.at[phase], sib_ss.at[phase], sib_rs.at[phase], (sibling, yz))
-        sent.append((sib_s.at[phase], sib_ss.at[phase]))
+            total = total + half_r[q].astype(F32)
+        sib_s[...] = total
+        send(sib_s, sib_r, one_ss.at[2], one_rs.at[2], (sibling, yz))
+        sent.append((sib_s, one_ss.at[2]))
         own = pl.ds(pl.multiple_of(core * HALF, HALF), HALF)
         other = pl.ds(pl.multiple_of((1 - core) * HALF, HALF), HALF)
         picked = dot(total.astype(BF16), near_inverse[own, :])
-        wait_bytes(sib_r.at[phase], sib_rs.at[phase])
-        picked = picked + dot(sib_r[phase].astype(BF16), near_inverse[other, :])
+        rhs[:, own] = total
+        wait_bytes(sib_r, one_rs.at[2])
+        remote = sib_r[...]
+        picked = picked + dot(remote.astype(BF16), near_inverse[other, :])
+        rhs[:, other] = remote
+        return dot(picked.astype(BF16), near[...])
+
+    def add_up(arrived):
+        return sum(arrived[q] for q in range(1, RING)) + arrived[0]
+
+    def parts_start(phase, image):
+        hi, lo = split(image)
+        both = dot(jnp.concatenate([hi, lo], axis=0), near_t[...])
+        hi, lo = split(both[0:CASES] + both[CASES:])
+        both = dot(jnp.concatenate([hi, lo], axis=0), chosen_t[...])
+        out = both[0:CASES] + both[CASES:]
+        for b in range(8):
+            for h in range(2):
+                part_s[phase, 2 * b + h] = out[8 * h : 8 * h + 8, b * LANES : (b + 1) * LANES]
+        part_r[phase, pl.ds(yz, 1)] = part_s[phase, pl.ds(yz, 1)]
+        arrivals = part_r.at[phase, pl.ds(0, 15)]
+        to_peers(lambda q: part_s.at[phase, q], part_r.at[phase, yz], arrivals, part_ss.at[phase], part_rs.at[phase])
+
+    def sums_start(phase):
+        wait_bytes(part_r.at[phase, pl.ds(0, 15)], part_rs.at[phase])
+        tile = add_up([part_r[phase, q] for q in range(RING)])
+        sum_s[phase] = tile
+        sum_r[phase, pl.ds(gx, 1)] = tile[None]
+        arrivals = sum_r.at[phase, pl.ds(0, 15)]
+        to_columns(sum_s.at[phase], sum_r.at[phase, gx], arrivals, sum_ss.at[phase], sum_rs.at[phase])
+
+    def all_start(phase):
+        wait_bytes(sum_r.at[phase, pl.ds(0, 15)], sum_rs.at[phase])
+        tile = add_up([sum_r[phase, g] for g in range(RING)])
+        all_s[phase] = tile
+        all_r[phase, pl.ds(yz, 1)] = tile[None]
+        arrivals = all_r.at[phase, pl.ds(0, 15)]
+        to_peers(lambda q: all_s.at[phase], all_r.at[phase, yz], arrivals, all_ss.at[phase], all_rs.at[phase])
+
+    def all_finish(phase):
+        wait_bytes(all_r.at[phase, pl.ds(0, 15)], all_rs.at[phase])
+        tiles = [jnp.concatenate([all_r[phase, 2 * b], all_r[phase, 2 * b + 1]], axis=0) for b in range(8)]
+        return jnp.concatenate(tiles, axis=1)
+
+    def coarse_part(values):
+        picked = dot(values.astype(BF16), near_inverse[...])
         return dot(picked.astype(BF16), near[...])
 
     def grams(phase, z, others):
@@ -295,9 +329,17 @@
         arrivals = gram_r.at[phase, pl.ds(0, 15)]
         to_peers(lambda q: gram_s.at[phase], gram_r.at[phase, yz], arrivals, gram_ss.at[phase], gram_rs.at[phase])
 
-    def grams_layer(phase):
+    def rings_start(phase):
         wait_bytes(gram_r.at[phase, pl.ds(0, 15)], gram_rs.at[phase])
-        return sum(gram_r[phase, q] for q in range(1, RING)) + gram_r[phase, 0]
+        layer = add_up([gram_r[phase, q] for q in range(RING)])
+        ring_s[phase] = layer
+        ring_r[phase, pl.ds(gx, 1)] = layer[None]
+        arrivals = ring_r.at[phase, pl.ds(0, 15)]
+        to_columns(ring_s.at[phase], ring_r.at[phase, gx], arrivals, ring_ss.at[phase], ring_rs.at[phase])
+
+    def rings_finish(phase):
+        wait_bytes(ring_r.at[phase, pl.ds(0, 15)], ring_rs.at[phase])
+        return unfold(add_up([ring_r[phase, g] for g in range(RING)]))
 
     for phase in range(3):
         slot_r[phase, pl.ds(yz, 1)] = jnp.zeros((1, CASES, LANES), BF16)
@@ -313,8 +355,8 @@
     pl.semaphore_wait(barrier, len(peers) + len(columns))
 
     exchange_send(0, slot_s, slot_r, face_r, slot_ss, slot_rs, face_ss, face_rs)
-    to_columns(pidx_s, pidx_rc.at[gx], pidx_rc.at[pl.ds(0, 15)], px_ss.at[0], px_rs.at[0])
-    to_peers(lambda q: pidx_s, pidx_rp.at[yz], pidx_rp.at[pl.ds(0, 15)], px_ss.at[1], px_rs.at[1])
+    to_columns(pidx_s, pidx_rc.at[gx], pidx_rc.at[pl.ds(0, 15)], one_ss.at[3], one_rs.at[3])
+    to_peers(lambda q: pidx_s, pidx_rp.at[yz], pidx_rp.at[pl.ds(0, 15)], one_ss.at[4], one_rs.at[4])
     idx_cols = jnp.transpose(idx[...].astype(F32))
     lane_iota = iota((LANES, IFACE), 1).astype(F32)
     for b in range(TILES):
@@ -331,30 +373,29 @@
     res = loads[...] + exchange_finish(0)
     weighted = weight[...] * res
     mine = coarse_terms(weighted)
-    col_s[0, 0] = mine
-    col_r[0, pl.ds(gx, 1), 0] = mine[None]
-    columns_start(0, 1)
+    col_s[...] = mine
+    col_r[pl.ds(gx, 1)] = mine[None]
+    to_columns(col_s, col_r.at[gx], col_r.at[pl.ds(0, 15)], one_ss.at[0], one_rs.at[0])
     own_smooth = smooth_start(0, weighted)
     res_out[...] = res
 
-    wait_bytes(pidx_rc.at[pl.ds(0, 15)], px_rs.at[0])
+    wait_bytes(pidx_rc.at[pl.ds(0, 15)], one_rs.at[3])
     owners = jnp.transpose(pack([pidx_rc[g] for g in range(RING)])[0:8])
     half_lane = (iota((PACKED, HALF), 1) + core * HALF).astype(F32)
     spread[...] = jnp.where(owners[:, 0:1] == half_lane, 1.0, 0.0).astype(BF16)
-    columns_wait(0, 1)
-    packed = pack([col_r[0, g, 0] for g in range(RING)])
-    coarse_start(0, packed)
-    terms0[...] = packed
-
-    wait_bytes(pidx_rp.at[pl.ds(0, 15)], px_rs.at[1])
+
+    wait_bytes(pidx_rp.at[pl.ds(0, 15)], one_rs.at[4])
     across_primals = pack([pidx_rp[q] for q in range(RING)])[0:8]
     lower = pidx_rc[pl.ds(below, 1)][0]
     upper = pltpu.roll(pidx_rc[pl.ds(above, 1)][0], 32, 1)
     face_primals = jnp.where(lane8 < 32, lower, jnp.where(lane8 < 64, upper, -1.0))
-    near_row = jnp.concatenate([across_primals, face_primals], axis=1)[0:1]
-    chosen = jnp.where(iota((COARSE, EXT), 0).astype(F32) == near_row, 1.0, 0.0).astype(BF16)
+    near_row = jnp.concatenate([across_primals, face_primals], axis=1)
+    chosen = jnp.where(iota((COARSE, EXT), 0).astype(F32) == near_row[0:1], 1.0, 0.0).astype(BF16)
     loading[1].wait()
     near_inverse[...] = dot(cinv[...], chosen).astype(BF16)
+
+    wait_bytes(col_r.at[pl.ds(0, 15)], one_rs.at[0])
+    coarse_start(pack([col_r[g] for g in range(RING)]))
 
     parts = exchange_arrived(3, wide_r, wface_r, wide_rs, wface_rs)
     lane32 = iota((BLOCK, LANES), 1)
@@ -371,93 +412,77 @@
     near[16 * BLOCK : 18 * BLOCK, :] = dot(faces.astype(BF16), scatter[8 * LANES :, :]).astype(BF16)
     near[18 * BLOCK :, :] = jnp.zeros((EXT - 18 * BLOCK, IFACE), BF16)
     near[pl.ds(pl.multiple_of(yz * BLOCK, BLOCK), BLOCK), :] = scaled
+    near_t[...] = jnp.transpose(near[...].astype(F32)).astype(BF16)
+    near_col = jnp.transpose(near_row)
+    chosen_t[...] = jnp.where(near_col[:, 0:1] == iota((EXT, COARSE), 1).astype(F32), 1.0, 0.0).astype(BF16)
 
     own_smooth = own_smooth + smooth_finish(0)
     smooth[...] = own_smooth
     loading[2].wait()
-    z = own_smooth + coarse_finish(0)
+    z = own_smooth + coarse_finish()
 
     image = dot(z.astype(BF16), stiff[...])
+    parts_start(0, image)
+    grams(0, z, [(32, image), (48, weighted)])
     exchange_start(1, image.astype(BF16))
-    grams(0, z, [(32, image), (48, weighted)])
+    sums_start(0)
+    rings_start(0)
     image = image + exchange_finish(1)
-    weighted = weight[...] * image
-    mine = coarse_terms(weighted)
-    mine = jnp.where((lane8 % 64) < 32, mine, grams_layer(0))
-    col_s[1, 0] = mine
-    col_r[1, pl.ds(gx, 1), 0] = mine[None]
-    columns_start(1, 1)
-    own_smooth = smooth_start(1, weighted)
+    own_smooth = smooth_start(1, weight[...] * image)
     img[...] = image
-    columns_wait(1, 1)
-    tiles = [col_r[1, g, 0] for g in range(RING)]
-    first = unfold(sum(tiles[1:]) + tiles[0])
-    image_terms = pack(tiles)
+    pre_out[...] = z
+    all_start(0)
+    first = rings_finish(0)
     alpha = factor_t(eliminate(first, 32), 48)
-    packed = terms0[...] - apply_t(alpha, image_terms)
-    coarse_start(1, packed)
-    terms0[...] = packed
     res_out[...] = res_out[...] - apply_t(alpha, image)
     sol_out[...] = apply_t(alpha, z)
-    pre_out[...] = z
-    identity = jnp.where(lane16 - 64 == iota((CASES, LANES), 0), 1.0, 0.0)
-    inverse = eliminate(lanes_of(first, 48) + identity, 48)
     own_smooth = own_smooth + smooth_finish(1)
     img_smooth[...] = own_smooth
     own_smooth = smooth[...] - apply_t(alpha, own_smooth)
     smooth[...] = own_smooth
-    z = own_smooth + coarse_finish(1)
+    image_rhs = all_finish(0)
+    img_rhs[...] = image_rhs
+    coarse = rhs[...] - apply_t(alpha, image_rhs)
+    rhs[...] = coarse
+    z = own_smooth + coarse_part(coarse)
 
     image = dot(z.astype(BF16), stiff[...])
+    parts_start(1, image)
+    grams(1, z, [(0, weight[...] * img[...]), (32, image), (48, weight[...] * res_out[...])])
     exchange_start(2, image.astype(BF16))
-    grams(1, z, [(0, weight[...] * img[...]), (32, image), (48, weight[...] * res_out[...])])
+    identity = jnp.where(lane16 - 64 == iota((CASES, LANES), 0), 1.0, 0.0)
+    inverse = factor_t(eliminate(lanes_of(first, 48) + identity, 48), 64)
+    sums_start(1)
+    rings_start(1)
     image = image + exchange_finish(2)
-    weighted = weight[...] * image
-    mine = coarse_terms(weighted)
-    layer = grams_layer(1)
-    mine = jnp.where((lane8 % 64) < 32, mine, layer)
-    col_s[2, 0] = mine
-    col_s[2, 1] = layer
-    col_r[2, pl.ds(gx, 1), 0] = mine[None]
-    col_r[2, pl.ds(gx, 1), 1] = layer[None]
-    columns_start(2, 2)
-    own_smooth = smooth_start(2, weighted)
-    columns_wait(2, 2)
-    tiles = [col_r[2, g, 0] for g in range(RING)]
-    second = unfold(sum(tiles[1:]) + tiles[0])
-    cross = [col_r[2, g, 1] for g in range(RING)]
-    cross = unfold(sum(cross[1:]) + cross[0])
-    cross = jnp.concatenate([jnp.zeros((48, LANES), F32), cross, jnp.zeros((64, LANES), F32)], axis=0)
+    own_smooth = smooth_start(2, weight[...] * image)
+    all_start(1)
+    second = rings_finish(1)
+    cross = jnp.concatenate([jnp.zeros((48, LANES), F32), second, jnp.zeros((64, LANES), F32)], axis=0)
     cross_t = jnp.transpose(cross)[0:CASES, :]
-    beta = apply_t(factor_t(inverse, 64), second)
+    beta = apply_t(inverse, second)
     beta_t = factor_t(beta, 48)
     curve = apply_t(beta_t, cross_t + apply_t(factor_t(first, 32), beta))
     curve = curve + apply_t(factor_t(cross_t, 48), beta) + pltpu.roll(second, 16, 1)
     system = jnp.where(lane16 < 64, curve, pltpu.roll(second, 16, 1))
-    new_terms = pack(tiles) + apply_t(beta_t, image_terms)
     alpha = factor_t(eliminate(system, 48), 64)
-    coarse_start(2, terms0[...] - apply_t(alpha, new_terms))
+    own_smooth = own_smooth + smooth_finish(2) + apply_t(beta_t, img_smooth[...])
+    own_smooth = smooth[...] - apply_t(alpha, own_smooth)
     image = image + apply_t(beta_t, img[...])
     res_out[...] = res_out[...] - apply_t(alpha, image)
     direction = z + apply_t(beta_t, pre_out[...])
     sol_out[...] = sol_out[...] + apply_t(alpha, direction)
-    own_smooth = own_smooth + smooth_finish(2) + apply_t(beta_t, img_smooth[...])
-    own_smooth = smooth[...] - apply_t(alpha, own_smooth)
-    pre_out[...] = own_smooth + coarse_finish(2)
+    image_rhs = all_finish(1) + apply_t(beta_t, img_rhs[...])
+    pre_out[...] = own_smooth + coarse_part(rhs[...] - apply_t(alpha, image_rhs))
 
     for arrivals, ssem in sent:
         wait_bytes(arrivals, ssem)
 
 
-def hand_over(a, b, c, a_out, b_out, c_out, sems):
-    copies = [
-        pltpu.make_async_copy(src, dst, sems.at[i])
-        for i, (src, dst) in enumerate([(a, a_out), (b, b_out), (c, c_out)])
-    ]
-    for copy in copies:
-        copy.start()
-    for copy in copies:
-        copy.wait()
+def hand_over(a, b, c, a_out, b_out, c_out):
+    a_out[...] = a[...]
+    b_out[...] = b[...]
+    c_out[...] = c[...]
 
 
 def per_device(*args):
@@ -480,13 +505,16 @@
             pltpu.VMEM((CASES, IFACE), F32),
             pltpu.VMEM((PACKED, HALF), BF16),
             pltpu.VMEM((EXT, IFACE), BF16),
+            pltpu.VMEM((IFACE, EXT), BF16),
+            pltpu.VMEM((EXT, COARSE), BF16),
             pltpu.VMEM((COARSE, EXT), BF16),
             pltpu.VMEM((LANES, LANES), jnp.int32),
             pltpu.VMEM((24, LANES), jnp.int32),
             pltpu.VMEM((CASES, IFACE), F32),
-            pltpu.VMEM((CASES, PACKED), F32),
+            pltpu.VMEM((CASES, COARSE), F32),
             pltpu.VMEM((CASES, IFACE), F32),
             pltpu.VMEM((CASES, IFACE), F32),
+            pltpu.VMEM((CASES, COARSE), F32),
             pltpu.VMEM((3, TILES, CASES, LANES), BF16),
             pltpu.VMEM((3, RING, CASES, LANES), BF16),
             pltpu.VMEM((3, 2, 2, CASES, LANES), BF16),
@@ -495,20 +523,28 @@
             pltpu.VMEM((4, 2, 2, BLOCK, LANES), BF16),
             pltpu.VMEM((2, 8, LANES), F32),
             pltpu.VMEM((2, RING, 8, LANES), F32),
-            pltpu.VMEM((3, 2, 8, LANES), F32),
-            pltpu.VMEM((3, RING, 2, 8, LANES), F32),
-            pltpu.VMEM((3, CASES, HALF), BF16),
-            pltpu.VMEM((3, RING, CASES, HALF), BF16),
-            pltpu.VMEM((3, CASES, HALF), F32),
-            pltpu.VMEM((3, CASES, HALF), F32),
+            pltpu.VMEM((2, 8, LANES), F32),
+            pltpu.VMEM((2, RING, 8, LANES), F32),
+            pltpu.VMEM((8, LANES), F32),
+            pltpu.VMEM((RING, 8, LANES), F32),
+            pltpu.VMEM((CASES, HALF), BF16),
+            pltpu.VMEM((RING, CASES, HALF), BF16),
+            pltpu.VMEM((CASES, HALF), F32),
+            pltpu.VMEM((CASES, HALF), F32),
+            pltpu.VMEM((2, RING, 8, LANES), F32),
+            pltpu.VMEM((2, RING, 8, LANES), F32),
+            pltpu.VMEM((2, 8, LANES), F32),
+            pltpu.VMEM((2, RING, 8, LANES), F32),
+            pltpu.VMEM((2, 8, LANES), F32),
+            pltpu.VMEM((2, RING, 8, LANES), F32),
             pltpu.VMEM((8, LANES), F32),
             pltpu.VMEM((RING, 8, LANES), F32),
             pltpu.VMEM((RING, 8, LANES), F32),
             dma((3,)),
             dma((3,)), dma((3,)), dma((3,)), dma((3,)),
             dma((4,)), dma((4,)), dma((4,)), dma((4,)),
-            dma((2,)), dma((2,)), dma((3,)), dma((3,)),
-            dma((3,)), dma((3,)), dma((3,)), dma((3,)), dma((2,)), dma((2,)),
+            dma((2,)), dma((2,)), dma((2,)), dma((2,)), dma((2,)), dma((2,)), dma((2,)), dma((2,)),
+            dma((2,)), dma((2,)), dma((5,)), dma((5,)),
         ],
         compiler_params=pltpu.CompilerParams(
             collective_id=0, has_side_effects=True, vmem_limit_bytes=56 * 2**20
@@ -517,9 +553,8 @@
     return pl.pallas_call(
         hand_over,
         out_shape=(vector, vector, vector),
-        in_specs=[hbm, hbm, hbm],
-        out_specs=(hbm, hbm, hbm),
-        scratch_shapes=[dma((3,))],
+        in_specs=[vmem, vmem, vmem],
+        out_specs=(vmem, vmem, vmem),
         compiler_params=pltpu.CompilerParams(vmem_limit_bytes=60 * 2**20),
     )(*results)
 

time: 79.7 us -> 62.8 us (0.79)
  Pallas kernels: 78.8 us -> 62 us
    pallas_call x1, Pallas kernels: 71 us -> 60.4 us  [per_device(): pl.pallas_call(kernel, out_shape=(vector, vector, vector), in_specs=[vmem...]
    pallas_call x1, Pallas kernels: 7.83 us -> 1.65 us  [per_device(): pl.pallas_call(hand_over, out_shape=(vector, vector, vector), in_specs=[v...]
where the time goes in v3:
time: 62.8 us; the launch traced here: 62.7 us
  Pallas kernels  62 us (99%)
  between operations  0.64 us (1%)
    pallas_call x1, Pallas kernels, per_device(): pl.pallas_call(kernel, out_shape=(vector, vector, vector), in_specs=[vmem...  60.4 us
    pallas_call x1, Pallas kernels, per_device(): pl.pallas_call(hand_over, out_shape=(vector, vector, vector), in_specs=[v...  1.65 us

profile of v3, /device:TPU:1, one launch (start us, length us, event | category | flops | bytes accessed | tf_op | source)
XLA Modules:
  0.0 62.7 jit_solution(6304263975194810694)
XLA Ops:
  0.6 60.4 %shard_map.121 = (f32[16,1152]{1,0:T(8,128)}, f32[16,1152]{1,0:T(8,128)}, f32[16,1152]{1,0:T(8,128)}) custom-call(f32[16,1152]{1,0:T(8,128)} %loads.1, bf16[1152,1152]{1,0:T(8,128)(2,1)} %stiff_hbm.1, bf16[1152,1152]{1,0:T(8,128)(2,1)} %linv_hbm.1, bf16[24,1152]{1,0:T(8,128)(2,1)} %basis.1, bf16[1024,1024]{1,0:T(8,128)(2,1)} %cinv_hbm.1, s32[1,24]{1,0:T(1,128)} %primal.1, ...), custom_call_target="tpu_custom_call" | custom-call | tf_op jit(solution)/shard_map/pallas_call | solution.py:493
  61.0 1.6 %shard_map.122 = (f32[16,1152]{1,0:T(8,128)}, f32[16,1152]{1,0:T(8,128)}, f32[16,1152]{1,0:T(8,128)}) custom-call(f32[16,1152]{1,0:T(8,128)} %get-tuple-element.6.a, f32[16,1152]{1,0:T(8,128)} %get-tuple-element.7.b, f32[16,1152]{1,0:T(8,128)} %get-tuple-element.8.c), custom_call_target="tpu_custom_call" | custom-call | tf_op jit(solution)/shard_map/pallas_call | solution.py:553

commit v4 on v3

--- a/solution.py
+++ b/solution.py
@@ -103,13 +103,14 @@
 
 
 def kernel(
-    loads, stiff_hbm, linv_hbm, basis, cinv_hbm, primal, lcounts, lindex, acounts, aindex,
-    sol_out, res_out, pre_out,
-    stiff, linv, cinv, gather, scatter, basis_cols, weight, spread, near, near_t, chosen_t, near_inverse,
+    loads_hbm, stiff_hbm, linv_hbm, basis_hbm, cinv_hbm, primal_hbm, lcounts_hbm, lindex_hbm, acounts_hbm, aindex_hbm,
+    sol_hbm, res_hbm, pre_hbm,
+    loads, basis, primal, lcounts, lindex, acounts, aindex, sol_out, res_out, pre_out,
+    stiff, linv, cinv, gather, scatter, basis_cols, weight, spread, near, to_coarse, from_coarse, near_inverse,
     idx, lidx, smooth, rhs, img, img_smooth, img_rhs,
     slot_s, slot_r, face_r, wide_s, wide_r, wface_r, gram_s, gram_r, ring_s, ring_r, col_s, col_r,
     half_s, half_r, sib_s, sib_r, part_s, part_r, sum_s, sum_r, all_s, all_r, pidx_s, pidx_rp, pidx_rc,
-    load_sem, slot_ss, slot_rs, face_ss, face_rs, wide_ss, wide_rs, wface_ss, wface_rs,
+    load_sem, store_sem, slot_ss, slot_rs, face_ss, face_rs, wide_ss, wide_rs, wface_ss, wface_rs,
     gram_ss, gram_rs, ring_ss, ring_rs, part_ss, part_rs, sum_ss, sum_rs, all_ss, all_rs, one_ss, one_rs,
 ):
     gx, yz = lax.axis_index("gx"), lax.axis_index("yz")
@@ -131,11 +132,9 @@
     for q in columns:
         pl.semaphore_signal(barrier, 1, device_id=(q, yz), device_id_type=MESH)
 
-    loading = [
-        pltpu.make_async_copy(linv_hbm, linv, load_sem.at[0]),
-        pltpu.make_async_copy(cinv_hbm, cinv, load_sem.at[1]),
-        pltpu.make_async_copy(stiff_hbm, stiff, load_sem.at[2]),
-    ]
+    lists = [(primal_hbm, primal), (lcounts_hbm, lcounts), (lindex_hbm, lindex), (acounts_hbm, acounts), (aindex_hbm, aindex)]
+    order = [*lists, (loads_hbm, loads), (basis_hbm, basis), (linv_hbm, linv), (cinv_hbm, cinv), (stiff_hbm, stiff)]
+    loading = [pltpu.make_async_copy(src, dst, load_sem.at[i]) for i, (src, dst) in enumerate(order)]
     for copy in loading:
         copy.start()
 
@@ -162,6 +161,8 @@
     lane16 = iota((CASES, LANES), 1)
     idx[...] = jnp.full((LANES, LANES), -1, jnp.int32)
     lidx[...] = jnp.full((24, LANES), -1, jnp.int32)
+    for copy in loading[0:5]:
+        copy.wait()
     slot_lane = iota((1, SLOTS), 1)
     for q in range(RING):
         lidx[q : q + 1, 0:SLOTS] = jnp.where(slot_lane < acounts[0:1, q : q + 1], aindex[0, q : q + 1, :], -1)
@@ -272,9 +273,7 @@
 
     def parts_start(phase, image):
         hi, lo = split(image)
-        both = dot(jnp.concatenate([hi, lo], axis=0), near_t[...])
-        hi, lo = split(both[0:CASES] + both[CASES:])
-        both = dot(jnp.concatenate([hi, lo], axis=0), chosen_t[...])
+        both = dot(jnp.concatenate([hi, lo], axis=0), to_coarse[...])
         out = both[0:CASES] + both[CASES:]
         for b in range(8):
             for h in range(2):
@@ -305,8 +304,7 @@
         return jnp.concatenate(tiles, axis=1)
 
     def coarse_part(values):
-        picked = dot(values.astype(BF16), near_inverse[...])
-        return dot(picked.astype(BF16), near[...])
+        return dot(values.astype(BF16), from_coarse[...])
 
     def grams(phase, z, others):
         z_hi, z_lo = split(z)
@@ -350,6 +348,7 @@
     pidx_s[...] = primals
     pidx_rp[pl.ds(yz, 1)] = primals[None]
     pidx_rc[pl.ds(gx, 1)] = primals[None]
+    loading[5].wait()
     exchange_values(slot_s, 0, loads[...].astype(BF16))
 
     pl.semaphore_wait(barrier, len(peers) + len(columns))
@@ -362,13 +361,14 @@
     for b in range(TILES):
         scatter[b * LANES : (b + 1) * LANES, :] = jnp.where(idx_cols[:, b : b + 1] == lane_iota, 1.0, 0.0).astype(BF16)
     weight[...] = 1.0 / (1.0 + dot(jnp.ones((CASES, NSLOT), BF16), scatter[...]))
+    loading[6].wait()
     basis_f32 = basis[...].astype(F32)
     basis_pad = jnp.concatenate([basis_f32, jnp.zeros((LANES - PRIMAL, IFACE), F32)], axis=0)
     basis_cols[...] = jnp.transpose(basis_pad).astype(BF16)
     scaled = jnp.concatenate([weight[...] * basis_pad[0:CASES], weight[...] * basis_pad[CASES:BLOCK]], axis=0)
     scaled = scaled.astype(BF16)
     wide_start(3, scaled)
-    loading[0].wait()
+    loading[7].wait()
 
     res = loads[...] + exchange_finish(0)
     weighted = weight[...] * res
@@ -391,7 +391,7 @@
     face_primals = jnp.where(lane8 < 32, lower, jnp.where(lane8 < 64, upper, -1.0))
     near_row = jnp.concatenate([across_primals, face_primals], axis=1)
     chosen = jnp.where(iota((COARSE, EXT), 0).astype(F32) == near_row[0:1], 1.0, 0.0).astype(BF16)
-    loading[1].wait()
+    loading[8].wait()
     near_inverse[...] = dot(cinv[...], chosen).astype(BF16)
 
     wait_bytes(col_r.at[pl.ds(0, 15)], one_rs.at[0])
@@ -412,19 +412,21 @@
     near[16 * BLOCK : 18 * BLOCK, :] = dot(faces.astype(BF16), scatter[8 * LANES :, :]).astype(BF16)
     near[18 * BLOCK :, :] = jnp.zeros((EXT - 18 * BLOCK, IFACE), BF16)
     near[pl.ds(pl.multiple_of(yz * BLOCK, BLOCK), BLOCK), :] = scaled
-    near_t[...] = jnp.transpose(near[...].astype(F32)).astype(BF16)
+    near_t = jnp.transpose(near[...].astype(F32)).astype(BF16)
     near_col = jnp.transpose(near_row)
-    chosen_t[...] = jnp.where(near_col[:, 0:1] == iota((EXT, COARSE), 1).astype(F32), 1.0, 0.0).astype(BF16)
+    chosen_t = jnp.where(near_col[:, 0:1] == iota((EXT, COARSE), 1).astype(F32), 1.0, 0.0).astype(BF16)
+    to_coarse[...] = dot(near_t, chosen_t).astype(BF16)
 
     own_smooth = own_smooth + smooth_finish(0)
     smooth[...] = own_smooth
-    loading[2].wait()
+    loading[9].wait()
     z = own_smooth + coarse_finish()
 
     image = dot(z.astype(BF16), stiff[...])
     parts_start(0, image)
     grams(0, z, [(32, image), (48, weighted)])
     exchange_start(1, image.astype(BF16))
+    from_coarse[...] = dot(near_inverse[...], near[...]).astype(BF16)
     sums_start(0)
     rings_start(0)
     image = image + exchange_finish(1)
@@ -473,10 +475,17 @@
     direction = z + apply_t(beta_t, pre_out[...])
     sol_out[...] = sol_out[...] + apply_t(alpha, direction)
     image_rhs = all_finish(1) + apply_t(beta_t, img_rhs[...])
+    results = [(sol_out, sol_hbm), (res_out, res_hbm), (pre_out, pre_hbm)]
+    storing = [pltpu.make_async_copy(src, dst, store_sem.at[i]) for i, (src, dst) in enumerate(results)]
+    storing[0].start()
+    storing[1].start()
     pre_out[...] = own_smooth + coarse_part(rhs[...] - apply_t(alpha, image_rhs))
 
+    storing[2].start()
     for arrivals, ssem in sent:
         wait_bytes(arrivals, ssem)
+    for copy in storing:
+        copy.wait()
 
 
 def hand_over(a, b, c, a_out, b_out, c_out):
@@ -487,15 +496,24 @@
 
 def per_device(*args):
     vector = jax.ShapeDtypeStruct((CASES, IFACE), F32)
-    vmem = pl.BlockSpec(memory_space=pltpu.VMEM)
     hbm = pl.BlockSpec(memory_space=pl.ANY)
     dma = pltpu.SemaphoreType.DMA
     results = pl.pallas_call(
         kernel,
         out_shape=(vector, vector, vector),
-        in_specs=[vmem, hbm, hbm, vmem, hbm, vmem, vmem, vmem, vmem, vmem],
-        out_specs=(vmem, vmem, vmem),
+        in_specs=[hbm] * 10,
+        out_specs=(hbm, hbm, hbm),
         scratch_shapes=[
+            pltpu.VMEM((CASES, IFACE), F32),
+            pltpu.VMEM((PRIMAL, IFACE), BF16),
+            pltpu.VMEM((1, PRIMAL), jnp.int32),
+            pltpu.VMEM((1, 2), jnp.int32),
+            pltpu.VMEM((1, 2, FACE), jnp.int32),
+            pltpu.VMEM((1, RING), jnp.int32),
+            pltpu.VMEM((1, RING, SLOTS), jnp.int32),
+            pltpu.VMEM((CASES, IFACE), F32),
+            pltpu.VMEM((CASES, IFACE), F32),
+            pltpu.VMEM((CASES, IFACE), F32),
             pltpu.VMEM((IFACE, IFACE), BF16),
             pltpu.VMEM((IFACE, IFACE), BF16),
             pltpu.VMEM((COARSE, COARSE), BF16),
@@ -505,8 +523,8 @@
             pltpu.VMEM((CASES, IFACE), F32),
             pltpu.VMEM((PACKED, HALF), BF16),
             pltpu.VMEM((EXT, IFACE), BF16),
-            pltpu.VMEM((IFACE, EXT), BF16),
-            pltpu.VMEM((EXT, COARSE), BF16),
+            pltpu.VMEM((IFACE, COARSE), BF16),
+            pltpu.VMEM((COARSE, IFACE), BF16),
             pltpu.VMEM((COARSE, EXT), BF16),
             pltpu.VMEM((LANES, LANES), jnp.int32),
             pltpu.VMEM((24, LANES), jnp.int32),
@@ -540,7 +558,7 @@
             pltpu.VMEM((8, LANES), F32),
             pltpu.VMEM((RING, 8, LANES), F32),
             pltpu.VMEM((RING, 8, LANES), F32),
-            dma((3,)),
+            dma((10,)), dma((3,)),
             dma((3,)), dma((3,)), dma((3,)), dma((3,)),
             dma((4,)), dma((4,)), dma((4,)), dma((4,)),
             dma((2,)), dma((2,)), dma((2,)), dma((2,)), dma((2,)), dma((2,)), dma((2,)), dma((2,)),
@@ -550,6 +568,7 @@
             collective_id=0, has_side_effects=True, vmem_limit_bytes=56 * 2**20
         ),
     )(*args)
+    vmem = pl.BlockSpec(memory_space=pltpu.VMEM)
     return pl.pallas_call(
         hand_over,
         out_shape=(vector, vector, vector),

time: 62.8 us -> 61.8 us (0.984)
  Pallas kernels: 62 us -> 61.1 us
    pallas_call x1, Pallas kernels: 60.4 us -> 59.4 us  [per_device(): pl.pallas_call(kernel, out_shape=(vector, vector, vector), in_specs=[hbm]...]
where the time goes in v4:
time: 61.8 us; the launch traced here: 61.7 us
  Pallas kernels  61.1 us (99%)
  between operations  0.64 us (1%)
    pallas_call x1, Pallas kernels, per_device(): pl.pallas_call(kernel, out_shape=(vector, vector, vector), in_specs=[hbm]...  59.4 us
    pallas_call x1, Pallas kernels, per_device(): pl.pallas_call(hand_over, out_shape=(vector, vector, vector), in_specs=[v...  1.65 us

profile of v4, /device:TPU:1, one launch (start us, length us, event | category | flops | bytes accessed | tf_op | source)
XLA Modules:
  0.0 61.7 jit_solution(14362889891724923348)
XLA Ops:
  0.6 59.4 %shard_map.121 = (f32[16,1152]{1,0:T(8,128)}, f32[16,1152]{1,0:T(8,128)}, f32[16,1152]{1,0:T(8,128)}) custom-call(f32[16,1152]{1,0:T(8,128)} %loads_hbm.1, bf16[1152,1152]{1,0:T(8,128)(2,1)} %stiff_hbm.1, bf16[1152,1152]{1,0:T(8,128)(2,1)} %linv_hbm.1, bf16[24,1152]{1,0:T(8,128)(2,1)} %basis_hbm.1, bf16[1024,1024]{1,0:T(8,128)(2,1)} %cinv_hbm.1, ...), custom_call_target="tpu_custom_call" | custom-call | tf_op jit(solution)/shard_map/pallas_call | solution.py:501
  60.0 1.6 %shard_map.122 = (f32[16,1152]{1,0:T(8,128)}, f32[16,1152]{1,0:T(8,128)}, f32[16,1152]{1,0:T(8,128)}) custom-call(f32[16,1152]{1,0:T(8,128)} %get-tuple-element.6.a, f32[16,1152]{1,0:T(8,128)} %get-tuple-element.7.b, f32[16,1152]{1,0:T(8,128)} %get-tuple-element.8.c), custom_call_target="tpu_custom_call" | custom-call | tf_op jit(solution)/shard_map/pallas_call | solution.py:572
